TPU v7x, 512 devices: a whole 4x4x16 slice. The times are simulated.
512 devices in a mesh: tm: 64 (over y, z_hi, x, core), head: 8 (over z_lo).
Axes of the slice: x: 4, y: 4, z: 16 (z_hi: 2, z_lo: 8; z = z_hi * 8 + z_lo), core: 2. Of those that a mesh axis runs over, the one named last changes fastest.
Arguments:
- queries: bfloat16 [64, 392, 1024], P('tm', None, 'head'), may hold values from -6 to 6
- key_tokens: bfloat16 [64, 392, 1024], P('tm', None, 'head'), may hold values from -6 to 6
- value_tokens: bfloat16 [64, 392, 1024], P('tm', None, 'head'), may hold values from -6 to 6
- out_weight: bfloat16 [1024, 1024], P('head'), may hold values from -0.1875 to 0.1875
- out_grad: bfloat16 [64, 392, 1024], P('tm'), may hold values from -6 to 6
- clip_starts: int32 [64], P('tm'), may hold values from 0 to 1, as said below
Outputs:
- projected: bfloat16 [64, 392, 1024], P('tm', 'head')
- grad_queries: bfloat16 [64, 392, 1024], P('tm', None, 'head')
- grad_keys: bfloat16 [64, 392, 1024], P('tm', None, 'head')
- grad_values: bfloat16 [64, 392, 1024], P('tm', None, 'head')
Inputs may be any that keep to these rules, and one draw needn't show every extreme that they name: `clip_starts`: the last 8 clips never begin a new video.
All inputs are finite; a program needn't handle non-finite values.
Results may differ from a plain program's by a relative error of at most 0.0087.
Values may be sent and summed in bfloat16 or wider, within the bound.
No kernel may reach another device: no remote copies, remote signals or barrier semaphores. Data moves between devices by JAX's collectives and lax.ppermute only.
A program may use at most 64 MiB of HBM per device.

v0:
```python
import jax
import jax.numpy as jnp
from jax import lax
from jax.sharding import PartitionSpec as P

HEAD_DIM = 64
POOL = 4
MEM = 8


def passed_along(block, axis, distance):
    devices = range(lax.axis_size(axis))
    route = [(i - distance, i) for i in devices if i - distance in devices]
    return lax.ppermute(block, axis, route)


def head_terms(query_part, key_part, value_part, column_mask, grad_part):
    scale = HEAD_DIM ** (-0.5)
    contract = (((1,), (1,)), ((), ()))
    across = (((0,), (0,)), ((), ()))
    scores = (
        lax.dot_general(query_part, key_part, contract, preferred_element_type=jnp.float32) * scale
    )
    scores = jnp.where(column_mask[None, :] > 0, scores, -1e30)
    peak = jnp.max(scores, axis=1, keepdims=True)
    expo = jnp.exp(scores - peak)
    probs = expo / jnp.sum(expo, axis=1, keepdims=True)
    weights = probs.astype(jnp.bfloat16)
    attended = jnp.dot(weights, value_part, preferred_element_type=jnp.float32).astype(jnp.bfloat16)
    grad_probs = lax.dot_general(
        grad_part, value_part, contract, preferred_element_type=jnp.float32
    )
    delta = jnp.sum(probs * grad_probs, axis=1, keepdims=True)
    grad_scores = (probs * (grad_probs - delta) * scale).astype(jnp.bfloat16)
    grad_query = jnp.dot(grad_scores, key_part, preferred_element_type=jnp.float32).astype(
        jnp.bfloat16
    )
    grad_key = lax.dot_general(grad_scores, query_part, across, preferred_element_type=jnp.float32)
    grad_value = lax.dot_general(weights, grad_part, across, preferred_element_type=jnp.float32)
    return (attended, grad_query, grad_key, grad_value)


def local(queries, key_tokens, value_tokens, out_weight, out_grad, clip_starts):
    query_rows = queries[0]
    key_rows = key_tokens[0]
    value_rows = value_tokens[0]
    token_count, local_width = query_rows.shape
    pooled_count = token_count // POOL
    local_heads = local_width // HEAD_DIM
    pooled_own = jnp.stack(
        [
            key_rows.astype(jnp.float32).reshape(pooled_count, POOL, local_width).mean(axis=1),
            value_rows.astype(jnp.float32).reshape(pooled_count, POOL, local_width).mean(axis=1),
        ]
    ).astype(jnp.bfloat16)
    keep = (1 - clip_starts[0]).astype(jnp.float32)
    slot_data = []
    slot_flags = []
    flag_pair = jnp.stack([jnp.ones((), jnp.float32), keep]).astype(jnp.bfloat16)
    running = keep
    for distance in range(1, MEM + 1):
        received, got_pair = passed_along((pooled_own, flag_pair), "tm", distance)
        slot_data.append(received)
        slot_flags.append(got_pair[0].astype(jnp.float32) * running)
        running = running * got_pair[1].astype(jnp.float32)
    memory = jnp.stack(slot_data)
    memory_keys = memory[:, 0].reshape(MEM * pooled_count, local_width)
    memory_values = memory[:, 1].reshape(MEM * pooled_count, local_width)
    key_ext = jnp.concatenate([key_rows, memory_keys], axis=0)
    value_ext = jnp.concatenate([value_rows, memory_values], axis=0)
    column_mask = jnp.concatenate(
        [jnp.ones((token_count,), jnp.float32), jnp.repeat(jnp.stack(slot_flags), pooled_count)]
    )
    grad_attended = lax.dot_general(
        out_grad[0], out_weight, (((1,), (1,)), ((), ())), preferred_element_type=jnp.float32
    ).astype(jnp.bfloat16)
    attended_parts, query_grads, key_grads, value_grads = ([], [], [], [])
    for head_number in range(local_heads):
        lower = head_number * HEAD_DIM
        upper = lower + HEAD_DIM
        outcome = head_terms(
            query_rows[:, lower:upper],
            key_ext[:, lower:upper],
            value_ext[:, lower:upper],
            column_mask,
            grad_attended[:, lower:upper],
        )
        attended_parts.append(outcome[0])
        query_grads.append(outcome[1])
        key_grads.append(outcome[2])
        value_grads.append(outcome[3])
    attended = jnp.concatenate(attended_parts, axis=1)
    grad_query_rows = jnp.concatenate(query_grads, axis=1)
    grad_key_ext = jnp.concatenate(key_grads, axis=1)
    grad_value_ext = jnp.concatenate(value_grads, axis=1)
    summed = lax.psum_scatter(
        jnp.dot(attended, out_weight, preferred_element_type=jnp.float32),
        "head",
        scatter_dimension=0,
        tiled=True,
    )
    projected = summed.astype(jnp.bfloat16)[None]
    memory_grads = jnp.stack(
        [
            grad_key_ext[token_count:].reshape(MEM, pooled_count, local_width),
            grad_value_ext[token_count:].reshape(MEM, pooled_count, local_width),
        ],
        axis=1,
    )
    returned = jnp.zeros((2, pooled_count, local_width), jnp.float32)
    for distance in range(1, MEM + 1):
        returned = returned + passed_along(
            memory_grads[distance - 1].astype(jnp.bfloat16), "tm", -distance
        ).astype(jnp.float32)
    grad_keys = (grad_key_ext[:token_count] + jnp.repeat(returned[0], POOL, axis=0) / POOL).astype(
        jnp.bfloat16
    )
    grad_values = (
        grad_value_ext[:token_count] + jnp.repeat(returned[1], POOL, axis=0) / POOL
    ).astype(jnp.bfloat16)
    return (projected, grad_query_rows[None], grad_keys[None], grad_values[None])


def solution(mesh):
    return jax.shard_map(
        local,
        mesh=mesh,
        in_specs=(
            P("tm", None, "head"),
            P("tm", None, "head"),
            P("tm", None, "head"),
            P("head", None),
            P("tm", None, None),
            P("tm"),
        ),
        out_specs=(
            P("tm", "head", None),
            P("tm", None, "head"),
            P("tm", None, "head"),
            P("tm", None, "head"),
        ),
        check_vma=False,
    )
```

profile of v0, /device:TPU:23, one launch (start us, length us, event | category | flops | bytes accessed | tf_op | source)
XLA Modules:
  0.0 323.9 jit_solution(9898168553057409962)
XLA Ops:
  1.4 15.4 %collective-permute-start.7 = (bf16[2]{0:T(256)(128)(2,1)S(1)}, bf16[2]{0:T(256)(128)(2,1)S(1)}, u32[]{:S(2)}, u32[]{:S(2)}) collective-permute-start(bf16[2]{0:T(256)(128)(2,1)S(1)} %pad_maximum_fusion.9), channel_id=1, source_target_pairs={{0,64},{8,72},{16,80},{24,88},{32,96},{40,104},{48,112},{56,120},{... | collective-permute-start | bytes 20 | tf_op jit(solution)/shard_map/ppermute | solution.py:14
  16.9 2.5 collective-permute-start.6
  19.4 13.3 %collective-permute-start.5 = (bf16[2]{0:T(256)(128)(2,1)S(1)}, bf16[2]{0:T(256)(128)(2,1)S(1)}, u32[]{:S(2)}, u32[]{:S(2)}) collective-permute-start(bf16[2]{0:T(256)(128)(2,1)S(1)} %pad_maximum_fusion.9), channel_id=1, source_target_pairs={{0,48},{8,56},{16,64},{24,72},{32,80},{40,88},{48,96},{56,104},{64... | collective-permute-start | bytes 20 | tf_op jit(solution)/shard_map/ppermute | solution.py:14
  32.7 2.2 collective-permute-start.4
  34.9 4.3 %collective-permute-start = (bf16[2]{0:T(256)(128)(2,1)S(1)}, bf16[2]{0:T(256)(128)(2,1)S(1)}, u32[]{:S(2)}, u32[]{:S(2)}) collective-permute-start(bf16[2]{0:T(256)(128)(2,1)S(1)} %pad_maximum_fusion.9), channel_id=1, source_target_pairs={{0,8},{8,16},{16,24},{24,32},{32,40},{40,48},{48,56},{56,64},{64,7... | collective-permute-start | bytes 20 | tf_op jit(solution)/shard_map/ppermute | solution.py:14
  43.3 1.4 convolution_convert_fusion
  44.7 2.3 collective-permute-start.1
  49.0 10.8 %collective-permute-start.2 = (bf16[2]{0:T(256)(128)(2,1)S(1)}, bf16[2]{0:T(256)(128)(2,1)S(1)}, u32[]{:S(2)}, u32[]{:S(2)}) collective-permute-start(bf16[2]{0:T(256)(128)(2,1)S(1)} %pad_maximum_fusion.9), channel_id=1, source_target_pairs={{0,24},{8,32},{16,40},{24,48},{32,56},{40,64},{48,72},{56,80},{64,... | collective-permute-start | bytes 20 | tf_op jit(solution)/shard_map/ppermute | solution.py:14
  61.0 14.4 %collective-permute-start.3 = (bf16[2]{0:T(256)(128)(2,1)S(1)}, bf16[2]{0:T(256)(128)(2,1)S(1)}, u32[]{:S(2)}, u32[]{:S(2)}) collective-permute-start(bf16[2]{0:T(256)(128)(2,1)S(1)} %pad_maximum_fusion.9), channel_id=1, source_target_pairs={{0,32},{8,40},{16,48},{24,56},{32,64},{40,72},{48,80},{56,88},{64,... | collective-permute-start | bytes 20 | tf_op jit(solution)/shard_map/ppermute | solution.py:14
  78.4 2.4 collective-permute-start.15
  82.7 2.6 collective-permute-start.14
  87.3 14.2 %collective-permute-start.13 = (bf16[2,98,128]{2,1,0:T(8,128)(2,1)S(1)}, bf16[2,98,128]{2,1,0:T(8,128)(2,1)S(1)}, u32[]{:S(2)}, u32[]{:S(2)}) collective-permute-start(bf16[2,98,128]{2,1,0:T(8,128)(2,1)S(1)} %pad_maximum_fusion.8), channel_id=1, source_target_pairs={{0,48},{8,56},{16,64},{24,72},{32,80},{40,88},{48,96},{56,104},{64... | collective-permute-start | bytes 150536 | tf_op jit(solution)/shard_map/ppermute | solution.py:14
  103.4 2.5 collective-permute-start.12
  108.5 14.9 %collective-permute-start.8 = (bf16[2,98,128]{2,1,0:T(8,128)(2,1)S(1)}, bf16[2,98,128]{2,1,0:T(8,128)(2,1)S(1)}, u32[]{:S(2)}, u32[]{:S(2)}) collective-permute-start(bf16[2,98,128]{2,1,0:T(8,128)(2,1)S(1)} %pad_maximum_fusion.8), channel_id=1, source_target_pairs={{0,8},{8,16},{16,24},{24,32},{32,40},{40,48},{48,56},{56,64},{64,7... | collective-permute-start | bytes 150536 | tf_op jit(solution)/shard_map/ppermute | solution.py:14
  123.7 1.3 collective-permute-done.8
  125.0 2.6 collective-permute-start.9
  127.6 2.2 collective-permute-done.9
  129.8 15.8 %collective-permute-start.10 = (bf16[2,98,128]{2,1,0:T(8,128)(2,1)S(1)}, bf16[2,98,128]{2,1,0:T(8,128)(2,1)S(1)}, u32[]{:S(2)}, u32[]{:S(2)}) collective-permute-start(bf16[2,98,128]{2,1,0:T(8,128)(2,1)S(1)} %pad_maximum_fusion.8), channel_id=1, source_target_pairs={{0,24},{8,32},{16,40},{24,48},{32,56},{40,64},{48,72},{56,80},{64,... | collective-permute-start | bytes 150536 | tf_op jit(solution)/shard_map/ppermute | solution.py:14
  146.9 15.7 %collective-permute-start.11 = (bf16[2,98,128]{2,1,0:T(8,128)(2,1)S(1)}, bf16[2,98,128]{2,1,0:T(8,128)(2,1)S(1)}, u32[]{:S(2)}, u32[]{:S(2)}) collective-permute-start(bf16[2,98,128]{2,1,0:T(8,128)(2,1)S(1)} %pad_maximum_fusion.8), channel_id=1, source_target_pairs={{0,32},{8,40},{16,48},{24,56},{32,64},{40,72},{48,80},{56,88},{64,... | collective-permute-start | bytes 150536 | tf_op jit(solution)/shard_map/ppermute | solution.py:14
  162.5 2.9 collective-permute-done.11
  184.0 2.3 collective-permute-start.17
  186.3 15.8 %collective-permute-start.18 = (bf16[2,98,128]{2,0,1:T(2,128)(2,1)}, bf16[2,98,128]{2,0,1:T(2,128)(2,1)}, u32[]{:S(2)}, u32[]{:S(2)}) collective-permute-start(bf16[2,98,128]{2,0,1:T(2,128)(2,1)} %bitcast.158), channel_id=1, source_target_pairs={{24,0},{32,8},{40,16},{48,24},{56,32},{64,40},{72,48},{80,56},{88,... | collective-permute-start | bytes 150536 | tf_op jit(solution)/shard_map/ppermute | solution.py:14
  202.1 15.4 %collective-permute-start.19 = (bf16[2,98,128]{2,0,1:T(2,128)(2,1)}, bf16[2,98,128]{2,0,1:T(2,128)(2,1)}, u32[]{:S(2)}, u32[]{:S(2)}) collective-permute-start(bf16[2,98,128]{2,0,1:T(2,128)(2,1)} %bitcast.157), channel_id=1, source_target_pairs={{32,0},{40,8},{48,16},{56,24},{64,32},{72,40},{80,48},{88,56},{96,... | collective-permute-start | bytes 150536 | tf_op jit(solution)/shard_map/ppermute | solution.py:14
  217.5 15.4 %collective-permute-start.21 = (bf16[2,98,128]{2,0,1:T(2,128)(2,1)}, bf16[2,98,128]{2,0,1:T(2,128)(2,1)}, u32[]{:S(2)}, u32[]{:S(2)}) collective-permute-start(bf16[2,98,128]{2,0,1:T(2,128)(2,1)} %bitcast.155), channel_id=1, source_target_pairs={{48,0},{56,8},{64,16},{72,24},{80,32},{88,40},{96,48},{104,56},{11... | collective-permute-start | bytes 150536 | tf_op jit(solution)/shard_map/ppermute | solution.py:14
  232.8 1.4 fusion.23
  234.3 41.4 %fusion = f32[56,1024]{1,0:T(8,128)} fusion(f32[392,1024]{1,0:T(8,128)S(1)} %fusion.23), kind=kCustom, calls=%all-reduce-scatter | all-reduce-scatter fusion | flops 458753 | bytes 1837056
  275.6 1.5 convolution_convert_fusion.2
  280.1 8.7 %collective-permute-start.20 = (bf16[2,98,128]{2,0,1:T(2,128)(2,1)S(1)}, bf16[2,98,128]{2,0,1:T(2,128)(2,1)S(1)}, u32[]{:S(2)}, u32[]{:S(2)}) collective-permute-start(bf16[2,98,128]{2,0,1:T(2,128)(2,1)S(1)} %bitcast.183), channel_id=1, source_target_pairs={{40,0},{48,8},{56,16},{64,24},{72,32},{80,40},{88,48},{96,56},{104... | collective-permute-start | bytes 150536 | tf_op jit(solution)/shard_map/ppermute | solution.py:14
  288.8 2.6 collective-permute-start.22
  291.4 9.6 %collective-permute-start.23 = (bf16[2,98,128]{2,0,1:T(2,128)(2,1)S(1)}, bf16[2,98,128]{2,0,1:T(2,128)(2,1)S(1)}, u32[]{:S(2)}, u32[]{:S(2)}) collective-permute-start(bf16[2,98,128]{2,0,1:T(2,128)(2,1)S(1)} %bitcast.181), channel_id=1, source_target_pairs={{64,0},{72,8},{80,16},{88,24},{96,32},{104,40},{112,48},{120,56},{... | collective-permute-start | bytes 150536 | tf_op jit(solution)/shard_map/ppermute | solution.py:14
  301.0 5.2 %collective-permute-start.16 = (bf16[2,98,128]{2,0,1:T(2,128)(2,1)S(1)}, bf16[2,98,128]{2,0,1:T(2,128)(2,1)S(1)}, u32[]{:S(2)}, u32[]{:S(2)}) collective-permute-start(bf16[2,98,128]{2,0,1:T(2,128)(2,1)S(1)} %bitcast.180), channel_id=1, source_target_pairs={{8,0},{16,8},{24,16},{32,24},{40,32},{48,40},{56,48},{64,56},{72,6... | collective-permute-start | bytes 150536 | tf_op jit(solution)/shard_map/ppermute | solution.py:14
  308.4 11.5 %collective-permute-done.16 = bf16[2,98,128]{2,0,1:T(2,128)(2,1)S(1)} collective-permute-done((bf16[2,98,128]{2,0,1:T(2,128)(2,1)S(1)}, bf16[2,98,128]{2,0,1:T(2,128)(2,1)S(1)}, u32[]{:S(2)}, u32[]{:S(2)}) %collective-permute-start.16) | collective-permute-done | bytes 50208 | tf_op jit(solution)/shard_map/ppermute | solution.py:14
  (128 shorter events, 37.6 us)
Async XLA Ops:
  0.6 42.7 %copy-start = (bf16[1,392,1024]{2,1,0:T(8,128)(2,1)S(1)}, bf16[1,392,1024]{2,1,0:T(8,128)(2,1)}, u32[]{:S(2)}) copy-start(bf16[1,392,1024]{2,1,0:T(8,128)(2,1)} %param.10) | copy-start | bytes 2408452
  1.4 107.0 %collective-permute-start.7 = (bf16[2]{0:T(256)(128)(2,1)S(1)}, bf16[2]{0:T(256)(128)(2,1)S(1)}, u32[]{:S(2)}, u32[]{:S(2)}) collective-permute-start(bf16[2]{0:T(256)(128)(2,1)S(1)} %pad_maximum_fusion.9), channel_id=1, source_target_pairs={{0,64},{8,72},{16,80},{24,88},{32,96},{40,104},{48,112},{56,120},{... | collective-permute-start | bytes 20 | tf_op jit(solution)/shard_map/ppermute | solution.py:14
  16.9 86.5 %collective-permute-start.6 = (bf16[2]{0:T(256)(128)(2,1)S(1)}, bf16[2]{0:T(256)(128)(2,1)S(1)}, u32[]{:S(2)}, u32[]{:S(2)}) collective-permute-start(bf16[2]{0:T(256)(128)(2,1)S(1)} %pad_maximum_fusion.9), channel_id=1, source_target_pairs={{0,56},{8,64},{16,72},{24,80},{32,88},{40,96},{48,104},{56,112},{6... | collective-permute-start | bytes 20 | tf_op jit(solution)/shard_map/ppermute | solution.py:14
  19.4 67.9 %collective-permute-start.5 = (bf16[2]{0:T(256)(128)(2,1)S(1)}, bf16[2]{0:T(256)(128)(2,1)S(1)}, u32[]{:S(2)}, u32[]{:S(2)}) collective-permute-start(bf16[2]{0:T(256)(128)(2,1)S(1)} %pad_maximum_fusion.9), channel_id=1, source_target_pairs={{0,48},{8,56},{16,64},{24,72},{32,80},{40,88},{48,96},{56,104},{64... | collective-permute-start | bytes 20 | tf_op jit(solution)/shard_map/ppermute | solution.py:14
  32.7 50.0 %collective-permute-start.4 = (bf16[2]{0:T(256)(128)(2,1)S(1)}, bf16[2]{0:T(256)(128)(2,1)S(1)}, u32[]{:S(2)}, u32[]{:S(2)}) collective-permute-start(bf16[2]{0:T(256)(128)(2,1)S(1)} %pad_maximum_fusion.9), channel_id=1, source_target_pairs={{0,40},{8,48},{16,56},{24,64},{32,72},{40,80},{48,88},{56,96},{64,... | collective-permute-start | bytes 20 | tf_op jit(solution)/shard_map/ppermute | solution.py:14
  34.9 9.8 %collective-permute-start = (bf16[2]{0:T(256)(128)(2,1)S(1)}, bf16[2]{0:T(256)(128)(2,1)S(1)}, u32[]{:S(2)}, u32[]{:S(2)}) collective-permute-start(bf16[2]{0:T(256)(128)(2,1)S(1)} %pad_maximum_fusion.9), channel_id=1, source_target_pairs={{0,8},{8,16},{16,24},{24,32},{32,40},{40,48},{48,56},{56,64},{64,7... | collective-permute-start | bytes 20 | tf_op jit(solution)/shard_map/ppermute | solution.py:14
  43.2 122.5 %copy-start.12 = (bf16[1,392,128]{2,1,0:T(8,128)(2,1)S(1)}, bf16[1,392,128]{2,1,0:T(8,128)(2,1)}, u32[]{:S(2)}) copy-start(bf16[1,392,128]{2,1,0:T(8,128)(2,1)} %param.6) | copy-start | bytes 301060
  43.2 122.5 %copy-start.13 = (bf16[1,392,128]{2,1,0:T(8,128)(2,1)S(1)}, bf16[1,392,128]{2,1,0:T(8,128)(2,1)}, u32[]{:S(2)}) copy-start(bf16[1,392,128]{2,1,0:T(8,128)(2,1)} %param.7) | copy-start | bytes 301060
  44.7 4.3 %collective-permute-start.1 = (bf16[2]{0:T(256)(128)(2,1)S(1)}, bf16[2]{0:T(256)(128)(2,1)S(1)}, u32[]{:S(2)}, u32[]{:S(2)}) collective-permute-start(bf16[2]{0:T(256)(128)(2,1)S(1)} %pad_maximum_fusion.9), channel_id=1, source_target_pairs={{0,16},{8,24},{16,32},{24,40},{32,48},{40,56},{48,64},{56,72},{64,... | collective-permute-start | bytes 20 | tf_op jit(solution)/shard_map/ppermute | solution.py:14
  49.0 12.0 %collective-permute-start.2 = (bf16[2]{0:T(256)(128)(2,1)S(1)}, bf16[2]{0:T(256)(128)(2,1)S(1)}, u32[]{:S(2)}, u32[]{:S(2)}) collective-permute-start(bf16[2]{0:T(256)(128)(2,1)S(1)} %pad_maximum_fusion.9), channel_id=1, source_target_pairs={{0,24},{8,32},{16,40},{24,48},{32,56},{40,64},{48,72},{56,80},{64,... | collective-permute-start | bytes 20 | tf_op jit(solution)/shard_map/ppermute | solution.py:14
  61.0 17.4 %collective-permute-start.3 = (bf16[2]{0:T(256)(128)(2,1)S(1)}, bf16[2]{0:T(256)(128)(2,1)S(1)}, u32[]{:S(2)}, u32[]{:S(2)}) collective-permute-start(bf16[2]{0:T(256)(128)(2,1)S(1)} %pad_maximum_fusion.9), channel_id=1, source_target_pairs={{0,32},{8,40},{16,48},{24,56},{32,64},{40,72},{48,80},{56,88},{64,... | collective-permute-start | bytes 20 | tf_op jit(solution)/shard_map/ppermute | solution.py:14
  78.4 87.1 %collective-permute-start.15 = (bf16[2,98,128]{2,1,0:T(8,128)(2,1)S(1)}, bf16[2,98,128]{2,1,0:T(8,128)(2,1)S(1)}, u32[]{:S(2)}, u32[]{:S(2)}) collective-permute-start(bf16[2,98,128]{2,1,0:T(8,128)(2,1)S(1)} %pad_maximum_fusion.8), channel_id=1, source_target_pairs={{0,64},{8,72},{16,80},{24,88},{32,96},{40,104},{48,112},{56,120},{... | collective-permute-start | bytes 150536 | tf_op jit(solution)/shard_map/ppermute | solution.py:14
  82.7 82.7 %collective-permute-start.14 = (bf16[2,98,128]{2,1,0:T(8,128)(2,1)S(1)}, bf16[2,98,128]{2,1,0:T(8,128)(2,1)S(1)}, u32[]{:S(2)}, u32[]{:S(2)}) collective-permute-start(bf16[2,98,128]{2,1,0:T(8,128)(2,1)S(1)} %pad_maximum_fusion.8), channel_id=1, source_target_pairs={{0,56},{8,64},{16,72},{24,80},{32,88},{40,96},{48,104},{56,112},{6... | collective-permute-start | bytes 150536 | tf_op jit(solution)/shard_map/ppermute | solution.py:14
  87.3 78.2 %collective-permute-start.13 = (bf16[2,98,128]{2,1,0:T(8,128)(2,1)S(1)}, bf16[2,98,128]{2,1,0:T(8,128)(2,1)S(1)}, u32[]{:S(2)}, u32[]{:S(2)}) collective-permute-start(bf16[2,98,128]{2,1,0:T(8,128)(2,1)S(1)} %pad_maximum_fusion.8), channel_id=1, source_target_pairs={{0,48},{8,56},{16,64},{24,72},{32,80},{40,88},{48,96},{56,104},{64... | collective-permute-start | bytes 150536 | tf_op jit(solution)/shard_map/ppermute | solution.py:14
  103.4 62.0 %collective-permute-start.12 = (bf16[2,98,128]{2,1,0:T(8,128)(2,1)S(1)}, bf16[2,98,128]{2,1,0:T(8,128)(2,1)S(1)}, u32[]{:S(2)}, u32[]{:S(2)}) collective-permute-start(bf16[2,98,128]{2,1,0:T(8,128)(2,1)S(1)} %pad_maximum_fusion.8), channel_id=1, source_target_pairs={{0,40},{8,48},{16,56},{24,64},{32,72},{40,80},{48,88},{56,96},{64,... | collective-permute-start | bytes 150536 | tf_op jit(solution)/shard_map/ppermute | solution.py:14
  108.5 16.5 %collective-permute-start.8 = (bf16[2,98,128]{2,1,0:T(8,128)(2,1)S(1)}, bf16[2,98,128]{2,1,0:T(8,128)(2,1)S(1)}, u32[]{:S(2)}, u32[]{:S(2)}) collective-permute-start(bf16[2,98,128]{2,1,0:T(8,128)(2,1)S(1)} %pad_maximum_fusion.8), channel_id=1, source_target_pairs={{0,8},{8,16},{16,24},{24,32},{32,40},{40,48},{48,56},{56,64},{64,7... | collective-permute-start | bytes 150536 | tf_op jit(solution)/shard_map/ppermute | solution.py:14
  125.0 4.9 %collective-permute-start.9 = (bf16[2,98,128]{2,1,0:T(8,128)(2,1)S(1)}, bf16[2,98,128]{2,1,0:T(8,128)(2,1)S(1)}, u32[]{:S(2)}, u32[]{:S(2)}) collective-permute-start(bf16[2,98,128]{2,1,0:T(8,128)(2,1)S(1)} %pad_maximum_fusion.8), channel_id=1, source_target_pairs={{0,16},{8,24},{16,32},{24,40},{32,48},{40,56},{48,64},{56,72},{64,... | collective-permute-start | bytes 150536 | tf_op jit(solution)/shard_map/ppermute | solution.py:14
  129.8 17.0 %collective-permute-start.10 = (bf16[2,98,128]{2,1,0:T(8,128)(2,1)S(1)}, bf16[2,98,128]{2,1,0:T(8,128)(2,1)S(1)}, u32[]{:S(2)}, u32[]{:S(2)}) collective-permute-start(bf16[2,98,128]{2,1,0:T(8,128)(2,1)S(1)} %pad_maximum_fusion.8), channel_id=1, source_target_pairs={{0,24},{8,32},{16,40},{24,48},{32,56},{40,64},{48,72},{56,80},{64,... | collective-permute-start | bytes 150536 | tf_op jit(solution)/shard_map/ppermute | solution.py:14
  146.9 18.5 %collective-permute-start.11 = (bf16[2,98,128]{2,1,0:T(8,128)(2,1)S(1)}, bf16[2,98,128]{2,1,0:T(8,128)(2,1)S(1)}, u32[]{:S(2)}, u32[]{:S(2)}) collective-permute-start(bf16[2,98,128]{2,1,0:T(8,128)(2,1)S(1)} %pad_maximum_fusion.8), channel_id=1, source_target_pairs={{0,32},{8,40},{16,48},{24,56},{32,64},{40,72},{48,80},{56,88},{64,... | collective-permute-start | bytes 150536 | tf_op jit(solution)/shard_map/ppermute | solution.py:14
  184.0 104.8 %collective-permute-start.17 = (bf16[2,98,128]{2,0,1:T(2,128)(2,1)}, bf16[2,98,128]{2,0,1:T(2,128)(2,1)}, u32[]{:S(2)}, u32[]{:S(2)}) collective-permute-start(bf16[2,98,128]{2,0,1:T(2,128)(2,1)} %bitcast.159), channel_id=1, source_target_pairs={{16,0},{24,8},{32,16},{40,24},{48,32},{56,40},{64,48},{72,56},{80,... | collective-permute-start | bytes 150536 | tf_op jit(solution)/shard_map/ppermute | solution.py:14
  186.3 105.1 %collective-permute-start.18 = (bf16[2,98,128]{2,0,1:T(2,128)(2,1)}, bf16[2,98,128]{2,0,1:T(2,128)(2,1)}, u32[]{:S(2)}, u32[]{:S(2)}) collective-permute-start(bf16[2,98,128]{2,0,1:T(2,128)(2,1)} %bitcast.158), channel_id=1, source_target_pairs={{24,0},{32,8},{40,16},{48,24},{56,32},{64,40},{72,48},{80,56},{88,... | collective-permute-start | bytes 150536 | tf_op jit(solution)/shard_map/ppermute | solution.py:14
  202.1 98.9 %collective-permute-start.19 = (bf16[2,98,128]{2,0,1:T(2,128)(2,1)}, bf16[2,98,128]{2,0,1:T(2,128)(2,1)}, u32[]{:S(2)}, u32[]{:S(2)}) collective-permute-start(bf16[2,98,128]{2,0,1:T(2,128)(2,1)} %bitcast.157), channel_id=1, source_target_pairs={{32,0},{40,8},{48,16},{56,24},{64,32},{72,40},{80,48},{88,56},{96,... | collective-permute-start | bytes 150536 | tf_op jit(solution)/shard_map/ppermute | solution.py:14
  217.5 90.9 %collective-permute-start.21 = (bf16[2,98,128]{2,0,1:T(2,128)(2,1)}, bf16[2,98,128]{2,0,1:T(2,128)(2,1)}, u32[]{:S(2)}, u32[]{:S(2)}) collective-permute-start(bf16[2,98,128]{2,0,1:T(2,128)(2,1)} %bitcast.155), channel_id=1, source_target_pairs={{48,0},{56,8},{64,16},{72,24},{80,32},{88,40},{96,48},{104,56},{11... | collective-permute-start | bytes 150536 | tf_op jit(solution)/shard_map/ppermute | solution.py:14
  275.6 30.6 %copy-start.14 = (bf16[392,64]{0,1:T(8,128)(2,1)S(1)}, bf16[392,64]{0,1:T(8,128)(2,1)}, u32[]{:S(2)}) copy-start(bf16[392,64]{0,1:T(8,128)(2,1)} %convolution_convert_fusion.1) | copy-start | bytes 150532
  275.6 31.4 %copy-start.9 = (f32[56,1024]{1,0:T(8,128)S(1)}, f32[56,1024]{1,0:T(8,128)}, u32[]{:S(2)}) copy-start(f32[56,1024]{1,0:T(8,128)} %fusion) | copy-start | bytes 688132
  275.6 45.6 %copy-start.2 = (f32[1176,64]{0,1:T(8,128)S(1)}, f32[1176,64]{0,1:T(8,128)}, u32[]{:S(2)}) copy-start(f32[1176,64]{0,1:T(8,128)} %copy-done.1) | copy-start | bytes 903172
  275.6 45.6 %copy-start.4 = (f32[1176,64]{0,1:T(8,128)S(1)}, f32[1176,64]{0,1:T(8,128)}, u32[]{:S(2)}) copy-start(f32[1176,64]{0,1:T(8,128)} %copy-done.3) | copy-start | bytes 903172
  280.1 27.0 %collective-permute-start.20 = (bf16[2,98,128]{2,0,1:T(2,128)(2,1)S(1)}, bf16[2,98,128]{2,0,1:T(2,128)(2,1)S(1)}, u32[]{:S(2)}, u32[]{:S(2)}) collective-permute-start(bf16[2,98,128]{2,0,1:T(2,128)(2,1)S(1)} %bitcast.183), channel_id=1, source_target_pairs={{40,0},{48,8},{56,16},{64,24},{72,32},{80,40},{88,48},{96,56},{104... | collective-permute-start | bytes 150536 | tf_op jit(solution)/shard_map/ppermute | solution.py:14
  288.8 19.6 %collective-permute-start.22 = (bf16[2,98,128]{2,0,1:T(2,128)(2,1)S(1)}, bf16[2,98,128]{2,0,1:T(2,128)(2,1)S(1)}, u32[]{:S(2)}, u32[]{:S(2)}) collective-permute-start(bf16[2,98,128]{2,0,1:T(2,128)(2,1)S(1)} %bitcast.182), channel_id=1, source_target_pairs={{56,0},{64,8},{72,16},{80,24},{88,32},{96,40},{104,48},{112,56},{1... | collective-permute-start | bytes 150536 | tf_op jit(solution)/shard_map/ppermute | solution.py:14
  291.4 17.0 %collective-permute-start.23 = (bf16[2,98,128]{2,0,1:T(2,128)(2,1)S(1)}, bf16[2,98,128]{2,0,1:T(2,128)(2,1)S(1)}, u32[]{:S(2)}, u32[]{:S(2)}) collective-permute-start(bf16[2,98,128]{2,0,1:T(2,128)(2,1)S(1)} %bitcast.181), channel_id=1, source_target_pairs={{64,0},{72,8},{80,16},{88,24},{96,32},{104,40},{112,48},{120,56},{... | collective-permute-start | bytes 150536 | tf_op jit(solution)/shard_map/ppermute | solution.py:14
  301.0 18.9 %collective-permute-start.16 = (bf16[2,98,128]{2,0,1:T(2,128)(2,1)S(1)}, bf16[2,98,128]{2,0,1:T(2,128)(2,1)S(1)}, u32[]{:S(2)}, u32[]{:S(2)}) collective-permute-start(bf16[2,98,128]{2,0,1:T(2,128)(2,1)S(1)} %bitcast.180), channel_id=1, source_target_pairs={{8,0},{16,8},{24,16},{32,24},{40,32},{48,40},{56,48},{64,56},{72,6... | collective-permute-start | bytes 150536 | tf_op jit(solution)/shard_map/ppermute | solution.py:14
  307.0 16.0 %collective-permute-start.24 = (bf16[49,1024]{1,0:T(8,128)(2,1)S(1)}, bf16[49,1024]{1,0:T(8,128)(2,1)S(1)}, u32[]{:S(2)}, u32[]{:S(2)}) collective-permute-start(bf16[49,1024]{1,0:T(8,128)(2,1)S(1)} %slice.186), channel_id=1, source_target_pairs={{0,1},{1,2},{2,3},{3,4},{4,5},{5,6},{6,7},{8,9},{9,10},{10,11},{11... | collective-permute-start | bytes 301064
  (8 other events, 67.7 us)
where the time goes:
time: 325 us; the launch traced here: 324 us
  starting transfers between devices  212 us (65%)
  blocking collectives  41.4 us (13%)
  waiting for transfers between devices  20.3 us (6%)
  local copies, waits for them, and re-layouts  19 us (6%)
  matrix products  12.1 us (4%)
  between operations  12 us (4%)
  other arithmetic  7.05 us (2%)
    ppermute x24, starting transfers between devices, passed_along(): return lax.ppermute(block, axis, route)  211 us
    unnamed x1, blocking collectives  41.4 us
    ppermute x24, waiting for transfers between devices, passed_along(): return lax.ppermute(block, axis, route)  20.3 us
    slice x9, local copies, waits for them, and re-layouts, local(): memory_grads[distance - 1].astype(jnp.bfloat16)  6.88 us
  transfers between devices with their start and end apart: 25, of which 7 were waited for; matrix products, arithmetic and copies ran while one was open for 19% of the time, Pallas kernels for 0%

commit v1 on v0

v1 whole, which is shorter than its diff:
```python
import jax
import jax.numpy as jnp
from jax import lax
from jax.experimental import pallas as pl
from jax.experimental.pallas import tpu as pltpu
from jax.sharding import PartitionSpec as P

HEAD_DIM = 64
POOL = 4
MEM = 8
SLOT = 112
TILE = 128
F32 = jnp.float32
BF16 = jnp.bfloat16
VMEM_LIMIT = 48 * 1024 * 1024


def dot(a, b):
    return jnp.dot(a, b, preferred_element_type=F32)


def dot_rows(a, b):
    return lax.dot_general(a, b, (((0,), (0,)), ((), ())), preferred_element_type=F32)


def dot_cols(a, b):
    return lax.dot_general(a, b, (((1,), (1,)), ((), ())), preferred_element_type=F32)


def call(body, outs, flops, moved, n_in, scalars=0, scratch=()):
    smem = pl.BlockSpec(memory_space=pltpu.SMEM)
    vmem = pl.BlockSpec(memory_space=pltpu.VMEM)
    return pl.pallas_call(
        body,
        out_shape=tuple(jax.ShapeDtypeStruct(s, d) for s, d in outs),
        in_specs=[smem] * scalars + [vmem] * n_in,
        out_specs=tuple(vmem for _ in outs),
        scratch_shapes=list(scratch),
        compiler_params=pltpu.CompilerParams(vmem_limit_bytes=VMEM_LIMIT),
        cost_estimate=pl.CostEstimate(flops=flops, bytes_accessed=moved, transcendentals=0),
    )


def pool_body(start_ref, k_ref, v_ref, out_ref):
    tokens = k_ref.shape[0]
    pooled = tokens // POOL
    row = lax.broadcasted_iota(jnp.int32, (SLOT, tokens), 0)
    col = lax.broadcasted_iota(jnp.int32, (SLOT, tokens), 1)
    matrix = jnp.where((col >> 2) == row, 1.0 / POOL, 0.0).astype(BF16)
    flag = start_ref[0].astype(F32)
    rows = lax.broadcasted_iota(jnp.int32, (SLOT, TILE), 0)
    out_ref[0] = jnp.where(rows < pooled, dot(matrix, k_ref[...]), flag).astype(BF16)
    out_ref[1] = dot(matrix, v_ref[...]).astype(BF16)


def stacked(x, width):
    tokens = x.shape[0]
    lane = lax.broadcasted_iota(jnp.int32, x.shape, 1)
    low = jnp.where(lane < HEAD_DIM, x, 0.0)
    high = jnp.where(lane < HEAD_DIM, 0.0, x)
    return jnp.concatenate([low, high, jnp.zeros((width - 2 * tokens, TILE), F32)], axis=0)


def unstacked(xt, tokens):
    x = xt.T
    lane = lax.broadcasted_iota(jnp.int32, (tokens, TILE), 1)
    return jnp.where(lane < HEAD_DIM, x[:tokens], x[tokens : 2 * tokens])


def own_body(q_ref, k_ref, v_ref, og_ref, w_ref, qs_ref, qst_ref, dos_ref, dost_ref, m_ref, l_ref, ot_ref):
    width = qs_ref.shape[0]
    q = stacked(q_ref[...].astype(F32) * HEAD_DIM**-0.5, width)
    qs_ref[...] = q.astype(BF16)
    qst = q.T.astype(BF16)
    qst_ref[...] = qst
    grad = dot_cols(og_ref[...], w_ref[...]).astype(BF16).astype(F32)
    grad = stacked(grad, width)
    dos_ref[...] = grad.astype(BF16)
    dost_ref[...] = grad.T.astype(BF16)
    scores = dot(k_ref[...], qst)
    peak = jnp.max(scores, axis=0, keepdims=True)
    expo = jnp.exp(scores - peak)
    m_ref[...] = peak
    l_ref[...] = jnp.sum(expo, axis=0, keepdims=True)
    ot_ref[...] = dot_rows(v_ref[...], expo.astype(BF16))


def memory_body(
    start_ref,
    q_ref, mem_ref, qs_ref, qst_ref, dos_ref, dost_ref, m_ref, l_ref, ot_ref,
    pay_ref, att_ref, mn_ref, inv_ref, delta_ref, dqt_ref,
    s_ref, p_ref, ds_ref, mk_ref, mv_ref,
):
    width = qs_ref.shape[0]
    tiles = width // TILE
    parts, rows_each = att_ref.shape[0], att_ref.shape[1]
    tokens = q_ref.shape[0]
    pooled = tokens // POOL
    position = lax.axis_index("tm")
    place = lax.rem(position, MEM)
    group = lax.div(position, MEM)
    started = [mem_ref[k, 0, pl.ds(96, 16), :].astype(F32)[8:16] for k in range(MEM)]
    ages = [lax.rem(place - k - 1 + 2 * MEM, MEM) for k in range(MEM)]
    own_start = start_ref[0].astype(F32)
    row = lax.broadcasted_iota(jnp.int32, (SLOT, TILE), 0)
    peaks = [None] * tiles
    for k in range(MEM):
        absent = jnp.where((group == 0) & (place <= k), 1.0, 0.0) + own_start
        blocked = jnp.full((8, TILE), absent, F32)
        for other in range(MEM):
            if other != k:
                blocked = blocked + started[other] * jnp.where(ages[other] < ages[k], 1.0, 0.0)
        mk_ref[pl.ds(k * SLOT, SLOT), :] = mem_ref[k, 0]
        mv_ref[pl.ds(k * SLOT, SLOT), :] = mem_ref[k, 1]
        scores = dot(mem_ref[k, 0], qst_ref[...])
        keep = (jnp.concatenate([blocked] * (SLOT // 8), axis=0) == 0.0) & (row < pooled)
        for t in range(tiles):
            piece = jnp.where(keep, scores[:, t * TILE : (t + 1) * TILE], -1e30)
            s_ref[pl.ds(k * SLOT, SLOT), pl.ds(t * TILE, TILE)] = piece
            top = jnp.max(piece.reshape(SLOT // 8, 8, TILE), axis=0)
            peaks[t] = top if peaks[t] is None else jnp.maximum(peaks[t], top)
    for t in range(tiles):
        lanes = pl.ds(t * TILE, TILE)
        own_peak = m_ref[:, lanes]
        peak = jnp.maximum(own_peak, jnp.max(peaks[t], axis=0, keepdims=True))
        total = None
        for k in range(MEM):
            rows = pl.ds(k * SLOT, SLOT)
            expo = jnp.exp(s_ref[rows, lanes] - peak)
            s_ref[rows, lanes] = expo
            part = jnp.sum(expo.reshape(SLOT // 8, 8, TILE), axis=0)
            total = part if total is None else total + part
        factor = jnp.exp(own_peak - peak)
        inverse = 1.0 / (jnp.sum(total, axis=0, keepdims=True) + l_ref[:, lanes] * factor)
        mn_ref[:, lanes] = peak
        inv_ref[:, lanes] = inverse
        for k in range(MEM):
            rows = pl.ds(k * SLOT, SLOT)
            probs = s_ref[rows, lanes] * inverse
            s_ref[rows, lanes] = probs
            p_ref[rows, lanes] = probs.astype(BF16)
        ot_ref_piece = ot_ref[:, lanes] * (factor * inverse)
        dqt_ref[:, lanes] = ot_ref_piece
    out_t = dqt_ref[...] + dot_rows(mv_ref[...], p_ref[...])
    delta = jnp.sum(out_t * dost_ref[...].astype(F32), axis=0, keepdims=True)
    delta_ref[...] = delta
    attended = unstacked(out_t, tokens)
    each = tokens // parts
    for part in range(parts):
        piece = attended[part * each : (part + 1) * each]
        piece = jnp.concatenate([piece, jnp.zeros((rows_each - each, TILE), F32)], axis=0)
        att_ref[part] = piece.astype(BF16)
    for k in range(MEM):
        rows = pl.ds(k * SLOT, SLOT)
        grad_probs = dot(mem_ref[k, 1], dost_ref[...])
        for t in range(tiles):
            lanes = pl.ds(t * TILE, TILE)
            piece = s_ref[rows, lanes] * (grad_probs[:, t * TILE : (t + 1) * TILE] - delta_ref[:, lanes])
            ds_ref[rows, lanes] = piece.astype(BF16)
        pay_ref[k, 0] = dot(ds_ref[rows, :], qs_ref[...]).astype(BF16)
        pay_ref[k, 1] = dot(p_ref[rows, :], dos_ref[...]).astype(BF16)
    dqt_ref[...] = dot_rows(mk_ref[...], ds_ref[...])


def back_body(
    k_ref, v_ref, qs_ref, qst_ref, dos_ref, dost_ref, m_ref, inv_ref, delta_ref, dqt_ref,
    gq_ref, own_ref,
):
    tokens = k_ref.shape[0]
    scores = dot(k_ref[...], qst_ref[...])
    probs = jnp.exp(scores - m_ref[...]) * inv_ref[...]
    grad_probs = dot(v_ref[...], dost_ref[...])
    grad_scores = (probs * (grad_probs - delta_ref[...])).astype(BF16)
    own_ref[0] = dot(grad_scores, qs_ref[...])
    own_ref[1] = dot(probs.astype(BF16), dos_ref[...])
    grad_t = (dqt_ref[...] + dot_rows(k_ref[...], grad_scores)) * HEAD_DIM**-0.5
    gq_ref[...] = unstacked(grad_t, tokens).astype(BF16)


def sum_body(got_ref, prev_ref, own_ref):
    place = lax.rem(lax.axis_index("tm"), MEM)
    prev = jnp.zeros(own_ref.shape, F32)
    own = jnp.zeros(own_ref.shape, F32)
    for i in range(MEM):
        block = got_ref[i].astype(F32)
        share = jnp.where(i <= place, 1.0, 0.0)
        prev = prev + block * share
        own = own + block * (1.0 - share)
    prev_ref[...] = prev.astype(BF16)
    own_ref[...] = own


def final_body(direct_ref, near_ref, far_ref, gk_ref, gv_ref):
    tokens = gk_ref.shape[0]
    row = lax.broadcasted_iota(jnp.int32, (tokens, SLOT), 0)
    col = lax.broadcasted_iota(jnp.int32, (tokens, SLOT), 1)
    matrix = jnp.where((row >> 2) == col, 1.0 / POOL, 0.0).astype(BF16)
    for which, out_ref in enumerate((gk_ref, gv_ref)):
        total = near_ref[which] + far_ref[which].astype(F32)
        high = total.astype(BF16)
        low = (total - high.astype(F32)).astype(BF16)
        spread = dot(matrix, high) + dot(matrix, low)
        out_ref[...] = (direct_ref[which] + spread).astype(BF16)


def project_body(att_ref, w_ref, mine_ref, other_ref):
    odd = lax.rem(lax.axis_index("head"), 2)
    parts = att_ref.shape[0]
    rows = mine_ref.shape[0]
    total = dot(att_ref[0], w_ref[0])
    for part in range(1, parts):
        total = total + dot(att_ref[part], w_ref[part])
    first, second = total[:rows], total[rows : 2 * rows]
    take = jnp.full(first.shape, odd, jnp.int32) == 1
    mine_ref[...] = jnp.where(take, second, first)
    other_ref[...] = jnp.where(take, first, second).astype(BF16)


def local(queries, key_tokens, value_tokens, out_weight, out_grad, clip_starts):
    q, k, v, grad = queries[0], key_tokens[0], value_tokens[0], out_grad[0]
    tokens = q.shape[0]
    clips = lax.axis_size("tm")
    heads = lax.axis_size("head")
    model = out_weight.shape[1]
    width = 7 * TILE
    groups = [list(range(s, s + MEM)) for s in range(0, clips, MEM)]
    sides = [list(range(s, heads, 2)) for s in range(2)]
    parts = heads // 2
    each = tokens // parts
    place = lax.axis_index("tm") % MEM

    weights = lax.all_gather(out_weight, "head", axis_index_groups=sides)

    (own,) = call(pool_body, [((2, SLOT, TILE), BF16)], 10**7, 10**6, 2, 1)(clip_starts, k, v)
    prev = lax.ppermute(own, "tm", [(c, c + MEM) for c in range(clips - MEM)])
    qs, qst, dos, dost, m_own, l_own, ot_own = call(
        own_body,
        [
            ((width, TILE), BF16), ((TILE, width), BF16), ((width, TILE), BF16), ((TILE, width), BF16),
            ((1, width), F32), ((1, width), F32), ((TILE, width), F32),
        ],
        2 * 10**9, 2 * 10**6, 5,
    )(q, k, v, grad, out_weight)
    later = jnp.arange(MEM)[:, None, None, None] > place
    outgoing = jnp.where(later, own[None], prev[None])
    memory = lax.all_to_all(outgoing, "tm", 0, 0, axis_index_groups=groups)
    payload, attended, m_all, inverse, delta, dqt = call(
        memory_body,
        [
            ((MEM, 2, SLOT, TILE), BF16), ((parts, SLOT, TILE), BF16),
            ((1, width), F32), ((1, width), F32), ((1, width), F32), ((TILE, width), F32),
        ],
        4 * 10**9, 4 * 10**6, 9, 1,
        [
            pltpu.VMEM((MEM * SLOT, width), F32), pltpu.VMEM((MEM * SLOT, width), BF16),
            pltpu.VMEM((MEM * SLOT, width), BF16), pltpu.VMEM((MEM * SLOT, TILE), BF16),
            pltpu.VMEM((MEM * SLOT, TILE), BF16),
        ],
    )(clip_starts, q, memory, qs, qst, dos, dost, m_own, l_own, ot_own)
    arrived = lax.all_to_all(payload, "tm", 0, 0, axis_index_groups=groups)
    rows_of_all = lax.all_to_all(attended, "head", 0, 0, axis_index_groups=sides)
    gq, direct = call(
        back_body, [((tokens, TILE), BF16), ((2, tokens, TILE), F32)], 2 * 10**9, 2 * 10**6, 10
    )(k, v, qs, qst, dos, dost, m_all, inverse, delta, dqt)
    back, near = call(
        sum_body, [((2, SLOT, TILE), BF16), ((2, SLOT, TILE), F32)], 10**6, 10**6, 1
    )(arrived)
    far = lax.ppermute(back, "tm", [(c + MEM, c) for c in range(clips - MEM)])
    mine, other = call(
        project_body, [((each // 2, model), F32), ((each // 2, model), BF16)], 10**9, 2 * 10**6, 2
    )(rows_of_all, weights)
    theirs = lax.ppermute(other, "head", [(h, h ^ 1) for h in range(heads)])
    projected = (mine + theirs.astype(F32)).astype(BF16)
    gk, gv = call(
        final_body, [((tokens, TILE), BF16), ((tokens, TILE), BF16)], 10**7, 10**6, 3
    )(direct, near, far)
    return projected[None], gq[None], gk[None], gv[None]


def solution(mesh):
    return jax.shard_map(
        local,
        mesh=mesh,
        in_specs=(
            P("tm", None, "head"),
            P("tm", None, "head"),
            P("tm", None, "head"),
            P("head", None),
            P("tm", None, None),
            P("tm"),
        ),
        out_specs=(
            P("tm", "head", None),
            P("tm", None, "head"),
            P("tm", None, "head"),
            P("tm", None, "head"),
        ),
        check_vma=False,
    )
```

time: 325 us -> 103 us (0.32)
  the two profiles are of different devices: /device:TPU:23 before, /device:TPU:12 now
where the time goes in v1:
time: 103 us
  starting transfers between devices  42 us (41%)
  waiting for transfers between devices  19.3 us (19%)
  between operations  14.8 us (14%)
  blocking collectives  12.3 us (12%)
  Pallas kernels  9.64 us (9%)
  local copies, waits for them, and re-layouts  3.03 us (3%)
  other arithmetic  1.56 us (2%)
    ppermute x1, starting transfers between devices, local(): prev = lax.ppermute(own, 'tm', [(c, c + MEM) for c in range(clips - MEM)])  15.7 us
    all_to_all x1, blocking collectives, local(): arrived = lax.all_to_all(payload, 'tm', 0, 0, axis_index_groups=groups)  12.3 us
    all_to_all x1, starting transfers between devices, local(): lax.all_to_all(attended, 'head', 0, 0, axis_index_groups=sides)  8.86 us
    all_to_all x1, waiting for transfers between devices, local(): lax.all_to_all(attended, 'head', 0, 0, axis_index_groups=sides)  7.58 us
    ppermute x1, starting transfers between devices, local(): far = lax.ppermute(back, 'tm', [(c + MEM, c) for c in range(clips - MEM)])  7.42 us
    all_to_all x1, waiting for transfers between devices, local(): memory = lax.all_to_all(outgoing, 'tm', 0, 0, axis_index_groups=groups)  5.51 us
    pallas_call x1, Pallas kernels, local(): call(memory_body, [((MEM, 2, SLOT, TILE), BF16), ((parts, SLOT, TILE), BF...  5.03 us
    ppermute x1, starting transfers between devices, local(): theirs = lax.ppermute(other, 'head', [(h, h ^ 1) for h in range(heads)])  4.98 us
  transfers between devices with their start and end apart: 6, of which 5 were waited for; matrix products, arithmetic and copies ran while one was open for 1% of the time, Pallas kernels for 9%

profile of v1, /device:TPU:12, one launch (start us, length us, event | category | flops | bytes accessed | tf_op | source)
XLA Modules:
  0.0 102.6 jit_solution(16592968249767927234)
XLA Ops:
  7.2 0.0 all-gather.3.cloned.1.call-start
  7.9 0.0 copy-start.1
  7.9 0.9 copy-done.1
  8.8 0.9 copy-done.3
  9.6 0.2 shard_map.93
  9.9 15.7 %collective-permute-start = (bf16[2,112,128]{2,1,0:T(8,128)(2,1)S(1)}, bf16[2,112,128]{2,1,0:T(8,128)(2,1)S(1)}, u32[]{:S(2)}, u32[]{:S(2)}) collective-permute-start(bf16[2,112,128]{2,1,0:T(8,128)(2,1)S(1)} %shard_map.93), channel_id=1, source_target_pairs={{0,64},{8,72},{16,80},{24,88},{32,96},{40,104},{48,112},{56,120},{... | collective-permute-start | bytes 172040 | tf_op jit(solution)/shard_map/ppermute | solution.py:235
  25.6 0.0 all-gather.3.cloned.1.call-update
  25.6 0.0 copy-start.6
  25.6 4.1 %collective-permute-done = bf16[2,112,128]{2,1,0:T(8,128)(2,1)S(1)} collective-permute-done((bf16[2,112,128]{2,1,0:T(8,128)(2,1)S(1)}, bf16[2,112,128]{2,1,0:T(8,128)(2,1)S(1)}, u32[]{:S(2)}, u32[]{:S(2)}) %collective-permute-start) | collective-permute-done | bytes 57376 | tf_op jit(solution)/shard_map/ppermute | solution.py:235
  29.8 0.9 broadcast_select_fusion
  30.6 4.9 %all-to-all-start = ((bf16[8,2,112,128]{3,2,1,0:T(8,128)(2,1)}), bf16[8,2,112,128]{3,2,1,0:T(8,128)(2,1)S(1)}, u32[]{:S(2)}, u32[]{:S(2)}) async-start(bf16[8,2,112,128]{3,2,1,0:T(8,128)(2,1)} %broadcast_select_fusion), calls=%async_computation | async-start | bytes 917504 | tf_op jit(solution)/shard_map/all_to_all | solution.py:246
  35.6 0.0 copy-done.6
  35.6 0.0 copy-done.2
  35.6 0.0 copy-done.4
  35.6 0.0 copy-done.7
  35.6 0.9 shard_map.94
  36.6 5.5 %all-to-all-done.mem_ref = bf16[8,2,112,128]{3,2,1,0:T(8,128)(2,1)S(1)} async-done(((bf16[8,2,112,128]{3,2,1,0:T(8,128)(2,1)}), bf16[8,2,112,128]{3,2,1,0:T(8,128)(2,1)S(1)}, u32[]{:S(2)}, u32[]{:S(2)}) %all-to-all-start) | async-done | bytes 458784 | tf_op jit(solution)/shard_map/all_to_all | solution.py:246
  42.1 5.0 %shard_map.95 = (bf16[8,2,112,128]{3,2,1,0:T(8,128)(2,1)S(1)}, bf16[4,112,128]{2,1,0:T(8,128)(2,1)}, f32[1,896]{1,0:T(1,128)S(1)}, f32[1,896]{1,0:T(1,128)S(1)},...) custom-call(s32[1]{0:T(128)S(6)} %copy.10.start_ref, bf16[392,128]{1,0:T(8,128)(2,1)S(1)} %bitcast.19, ...), custom_call_target="tpu_custom_call" | custom-call | flops 4000000000 | bytes 4000000 | tf_op jit(solution)/shard_map/pallas_call | solution.py:247
  47.1 12.3 %all_to_all.15.got_ref = bf16[8,2,112,128]{3,2,1,0:T(8,128)(2,1)S(1)} all-to-all(bf16[8,2,112,128]{3,2,1,0:T(8,128)(2,1)S(1)} %get-tuple-element.41), channel_id=1, replica_groups={{0,8,16,24,32,40,48,56},{64,72,80,88,96,104,112,120},{128,136,144,152,1..., dimensions={0} | all-to-all | bytes 917504 | tf_op jit(solution)/shard_map/all_to_all | solution.py:260
  59.4 8.9 %all-to-all-start.1 = ((bf16[4,112,128]{2,1,0:T(8,128)(2,1)}), bf16[4,112,128]{2,1,0:T(8,128)(2,1)S(1)}, u32[]{:S(2)}, u32[]{:S(2)}) async-start(bf16[4,112,128]{2,1,0:T(8,128)(2,1)} %get-tuple-element.32), calls=%async_computation.1 | async-start | bytes 229376 | tf_op jit(solution)/shard_map/all_to_all | solution.py:261
  68.3 0.2 shard_map.98
  68.5 7.4 %collective-permute-start.2 = (bf16[2,112,128]{2,1,0:T(8,128)(2,1)S(1)}, bf16[2,112,128]{2,1,0:T(8,128)(2,1)S(1)}, u32[]{:S(2)}, u32[]{:S(2)}) collective-permute-start(bf16[2,112,128]{2,1,0:T(8,128)(2,1)S(1)} %get-tuple-element.43), channel_id=1, source_target_pairs={{64,0},{72,8},{80,16},{88,24},{96,32},{104,40},{112,48},{120,56},{... | collective-permute-start | bytes 172040 | tf_op jit(solution)/shard_map/ppermute | solution.py:268
  75.9 7.6 %all-to-all-done.1.att_ref = bf16[4,112,128]{2,1,0:T(8,128)(2,1)S(1)} async-done(((bf16[4,112,128]{2,1,0:T(8,128)(2,1)}), bf16[4,112,128]{2,1,0:T(8,128)(2,1)S(1)}, u32[]{:S(2)}, u32[]{:S(2)}) %all-to-all-start.1) | async-done | bytes 114720 | tf_op jit(solution)/shard_map/all_to_all | solution.py:261
  83.5 1.5 %all-gather.3.cloned.1.call-done = bf16[512,1024]{1,0:T(8,128)(2,1)} async-done(((bf16[128,1024]{1,0:T(8,128)(2,1)}), bf16[512,1024]{1,0:T(8,128)(2,1)}) %all-gather.3.cloned.1.call-update) | async-done | bytes 1048592 | tf_op jit(solution)/shard_map/all_gather | solution.py:232
  85.0 1.2 %copy-done.5 = bf16[512,1024]{1,0:T(8,128)(2,1)S(1)} copy-done((bf16[512,1024]{1,0:T(8,128)(2,1)S(1)}, bf16[512,1024]{1,0:T(8,128)(2,1)}, u32[]{:S(2)}) %copy-start.5) | copy-done | bytes 1048600
  86.2 0.4 shard_map.96
  86.6 5.0 %collective-permute-start.1 = (bf16[49,1024]{1,0:T(8,128)(2,1)S(1)}, bf16[49,1024]{1,0:T(8,128)(2,1)S(1)}, u32[]{:S(2)}, u32[]{:S(2)}) collective-permute-start(bf16[49,1024]{1,0:T(8,128)(2,1)S(1)} %get-tuple-element.34), channel_id=1, source_target_pairs={{0,1},{1,0},{2,3},{3,2},{4,5},{5,4},{6,7},{7,6},{8,9},{9,8},{10,11... | collective-permute-start | bytes 301064 | tf_op jit(solution)/shard_map/ppermute | solution.py:272
  91.6 1.9 %shard_map.97 = (bf16[392,128]{1,0:T(8,128)(2,1)}, f32[2,392,128]{2,1,0:T(8,128)S(1)}) custom-call(bf16[392,128]{1,0:T(8,128)(2,1)S(1)} %bitcast.12, bf16[392,128]{1,0:T(8,128)(2,1)S(1)} %bitcast.15, bf16[896,128]{1,0:T(8,128)(2,1)S(1)} %get-tuple-element.25.qs_ref, bf16[128,896]{1,0:T(8,128)(2,1)S(1)} %get-tuple-element.26.qst_ref, ...), custom_call_target="tpu_custom_call" | custom-call | flops 2000000000 | bytes 2000000 | tf_op jit(solution)/shard_map/pallas_call | solution.py:262
  93.5 0.0 collective-permute-done.2.far_ref
  93.5 1.0 shard_map.99
  94.5 0.5 collective-permute-done.1
  95.0 0.7 fusion
  (8 shorter events, 0.0 us)
Async XLA Ops:
  7.2 77.8 %all-gather.3.cloned.1.call-start = ((), (), s32[]{:S(2)}) async-start(), calls=%async_computation.3 | async-start | bytes 1310720 | tf_op jit(solution)/shard_map/all_gather | solution.py:232
  7.9 0.9 copy-start.1
  8.8 0.9 copy-start.3
  9.9 19.9 %collective-permute-start = (bf16[2,112,128]{2,1,0:T(8,128)(2,1)S(1)}, bf16[2,112,128]{2,1,0:T(8,128)(2,1)S(1)}, u32[]{:S(2)}, u32[]{:S(2)}) collective-permute-start(bf16[2,112,128]{2,1,0:T(8,128)(2,1)S(1)} %shard_map.93), channel_id=1, source_target_pairs={{0,64},{8,72},{16,80},{24,88},{32,96},{40,104},{48,112},{56,120},{... | collective-permute-start | bytes 172040 | tf_op jit(solution)/shard_map/ppermute | solution.py:235
  25.6 10.0 %copy-start.6 = (bf16[1,392,1024]{2,1,0:T(8,128)(2,1)S(1)}, bf16[1,392,1024]{2,1,0:T(8,128)(2,1)}, u32[]{:S(2)}) copy-start(bf16[1,392,1024]{2,1,0:T(8,128)(2,1)} %param.10) | copy-start | bytes 2408452
  30.6 5.0 %copy-start = (bf16[128,1024]{1,0:T(8,128)(2,1)S(1)}, bf16[128,1024]{1,0:T(8,128)(2,1)}, u32[]{:S(2)}) copy-start(bf16[128,1024]{1,0:T(8,128)(2,1)} %w_ref.1) | copy-start | bytes 786436
  30.6 5.0 %copy-start.2 = (bf16[1,392,128]{2,1,0:T(8,128)(2,1)S(1)}, bf16[1,392,128]{2,1,0:T(8,128)(2,1)}, u32[]{:S(2)}) copy-start(bf16[1,392,128]{2,1,0:T(8,128)(2,1)} %param.7) | copy-start | bytes 301060
  30.6 5.0 %copy-start.4 = (bf16[1,392,128]{2,1,0:T(8,128)(2,1)S(1)}, bf16[1,392,128]{2,1,0:T(8,128)(2,1)}, u32[]{:S(2)}) copy-start(bf16[1,392,128]{2,1,0:T(8,128)(2,1)} %param.8) | copy-start | bytes 301060
  30.6 5.0 %copy-start.7 = (bf16[1,392,128]{2,1,0:T(8,128)(2,1)S(1)}, bf16[1,392,128]{2,1,0:T(8,128)(2,1)}, u32[]{:S(2)}) copy-start(bf16[1,392,128]{2,1,0:T(8,128)(2,1)} %param.6) | copy-start | bytes 301060
  30.6 11.4 %all-to-all-start = ((bf16[8,2,112,128]{3,2,1,0:T(8,128)(2,1)}), bf16[8,2,112,128]{3,2,1,0:T(8,128)(2,1)S(1)}, u32[]{:S(2)}, u32[]{:S(2)}) async-start(bf16[8,2,112,128]{3,2,1,0:T(8,128)(2,1)} %broadcast_select_fusion), calls=%async_computation | async-start | bytes 917504 | tf_op jit(solution)/shard_map/all_to_all | solution.py:246
  59.4 24.1 %all-to-all-start.1 = ((bf16[4,112,128]{2,1,0:T(8,128)(2,1)}), bf16[4,112,128]{2,1,0:T(8,128)(2,1)S(1)}, u32[]{:S(2)}, u32[]{:S(2)}) async-start(bf16[4,112,128]{2,1,0:T(8,128)(2,1)} %get-tuple-element.32), calls=%async_computation.1 | async-start | bytes 229376 | tf_op jit(solution)/shard_map/all_to_all | solution.py:261
  68.5 25.0 %collective-permute-start.2 = (bf16[2,112,128]{2,1,0:T(8,128)(2,1)S(1)}, bf16[2,112,128]{2,1,0:T(8,128)(2,1)S(1)}, u32[]{:S(2)}, u32[]{:S(2)}) collective-permute-start(bf16[2,112,128]{2,1,0:T(8,128)(2,1)S(1)} %get-tuple-element.43), channel_id=1, source_target_pairs={{64,0},{72,8},{80,16},{88,24},{96,32},{104,40},{112,48},{120,56},{... | collective-permute-start | bytes 172040 | tf_op jit(solution)/shard_map/ppermute | solution.py:268
  85.0 1.2 %copy-start.5 = (bf16[512,1024]{1,0:T(8,128)(2,1)S(1)}, bf16[512,1024]{1,0:T(8,128)(2,1)}, u32[]{:S(2)}) copy-start(bf16[512,1024]{1,0:T(8,128)(2,1)} %all-gather.3.cloned.1.call-done) | copy-start | bytes 3145732
  86.6 8.4 %collective-permute-start.1 = (bf16[49,1024]{1,0:T(8,128)(2,1)S(1)}, bf16[49,1024]{1,0:T(8,128)(2,1)S(1)}, u32[]{:S(2)}, u32[]{:S(2)}) collective-permute-start(bf16[49,1024]{1,0:T(8,128)(2,1)S(1)} %get-tuple-element.34), channel_id=1, source_target_pairs={{0,1},{1,0},{2,3},{3,2},{4,5},{5,4},{6,7},{7,6},{8,9},{9,8},{10,11... | collective-permute-start | bytes 301064 | tf_op jit(solution)/shard_map/ppermute | solution.py:272
Sparse Core Ops, SparseCore 0:
  25.7 59.2 all-gather.2

commit v2 on v1

v2 whole, which is shorter than its diff:
```python
import jax
import jax.numpy as jnp
from jax import lax
from jax.experimental import pallas as pl
from jax.experimental.pallas import tpu as pltpu
from jax.sharding import PartitionSpec as P

HEAD_DIM = 64
POOL = 4
MEM = 8
SLOT = 112
TILE = 128
F32 = jnp.float32
BF16 = jnp.bfloat16
VMEM_LIMIT = 20 * 1024 * 1024


def dot(a, b):
    return jnp.dot(a, b, preferred_element_type=F32)


def dot_rows(a, b):
    return lax.dot_general(a, b, (((0,), (0,)), ((), ())), preferred_element_type=F32)


def dot_cols(a, b):
    return lax.dot_general(a, b, (((1,), (1,)), ((), ())), preferred_element_type=F32)


def call(body, outs, flops, moved, n_in, scalars=0, scratch=(), spaces=None, limit=VMEM_LIMIT):
    smem = pl.BlockSpec(memory_space=pltpu.SMEM)
    vmem = pl.BlockSpec(memory_space=pltpu.VMEM)
    return pl.pallas_call(
        body,
        out_shape=tuple(jax.ShapeDtypeStruct(s, d) for s, d in outs),
        in_specs=[smem] * scalars + [
            pl.BlockSpec(memory_space=space) for space in spaces or [pltpu.VMEM] * n_in
        ],
        out_specs=tuple(vmem for _ in outs),
        scratch_shapes=list(scratch),
        compiler_params=pltpu.CompilerParams(vmem_limit_bytes=limit),
        cost_estimate=pl.CostEstimate(flops=flops, bytes_accessed=moved, transcendentals=0),
    )


def pool_body(start_ref, k_hbm, v_hbm, out_ref, k_ref, v_ref, sems):
    loads = [
        pltpu.make_async_copy(k_hbm, k_ref, sems.at[0]),
        pltpu.make_async_copy(v_hbm, v_ref, sems.at[1]),
    ]
    for load in loads:
        load.start()
    tokens = k_ref.shape[0]
    pooled = tokens // POOL
    row = lax.broadcasted_iota(jnp.int32, (SLOT, tokens), 0)
    col = lax.broadcasted_iota(jnp.int32, (SLOT, tokens), 1)
    matrix = jnp.where((col >> 2) == row, 1.0 / POOL, 0.0).astype(BF16)
    flag = start_ref[0].astype(F32)
    for load in loads:
        load.wait()
    rows = lax.broadcasted_iota(jnp.int32, (SLOT, TILE), 0)
    out_ref[0] = jnp.where(rows < pooled, dot(matrix, k_ref[...]), flag).astype(BF16)
    out_ref[1] = dot(matrix, v_ref[...]).astype(BF16)


def choose_body(own_ref, prev_ref, out_ref):
    place = lax.rem(lax.axis_index("tm"), MEM)
    own = own_ref[...].astype(F32)
    prev = prev_ref[...].astype(F32)
    for k in range(MEM):
        ours = jnp.full(own.shape, place, jnp.int32) < k
        out_ref[k] = jnp.where(ours, own, prev).astype(BF16)


def stacked(x, width):
    tokens = x.shape[0]
    lane = lax.broadcasted_iota(jnp.int32, x.shape, 1)
    low = jnp.where(lane < HEAD_DIM, x, 0.0)
    high = jnp.where(lane < HEAD_DIM, 0.0, x)
    return jnp.concatenate([low, high, jnp.zeros((width - 2 * tokens, TILE), F32)], axis=0)


def unstacked(xt, tokens):
    x = xt.T
    lane = lax.broadcasted_iota(jnp.int32, (tokens, TILE), 1)
    return jnp.where(lane < HEAD_DIM, x[:tokens], x[tokens : 2 * tokens])


def prepare_body(og_ref, w_ref, grad_ref, dost_ref):
    width = dost_ref.shape[1]
    grad = dot_cols(og_ref[...], w_ref[...]).astype(BF16)
    grad_ref[...] = grad
    dost_ref[...] = stacked(grad.astype(F32), width).T.astype(BF16)


def own_body(q_ref, k_ref, v_ref, m_ref, l_ref, ot_ref):
    width = ot_ref.shape[1]
    qs = stacked(q_ref[...].astype(F32) * HEAD_DIM**-0.5, width).astype(BF16)
    scores = dot_cols(k_ref[...], qs)
    peak = jnp.max(scores, axis=0, keepdims=True)
    expo = jnp.exp(scores - peak)
    m_ref[...] = peak
    l_ref[...] = jnp.sum(expo, axis=0, keepdims=True)
    ot_ref[...] = dot_rows(v_ref[...], expo.astype(BF16))


def memory_body(
    start_ref,
    q_ref, grad_ref, mem_ref, m_ref, l_ref, dost_hbm, ot_hbm,
    pay_ref, keep_ref, give_ref, mn_ref, inv_ref, delta_ref, dqt_ref,
    s_ref, p_ref, ds_ref, mk_ref, mv_ref, qs_ref, dos_ref, dost_ref, ot_ref, sems,
):
    width = qs_ref.shape[0]
    loads = [
        pltpu.make_async_copy(dost_hbm, dost_ref, sems.at[0]),
        pltpu.make_async_copy(ot_hbm, ot_ref, sems.at[1]),
    ]
    for load in loads:
        load.start()
    qs_ref[...] = stacked(q_ref[...].astype(F32) * HEAD_DIM**-0.5, width).astype(BF16)
    dos_ref[...] = stacked(grad_ref[...].astype(F32), width).astype(BF16)
    tiles = width // TILE
    tokens = q_ref.shape[0]
    pooled = tokens // POOL
    position = lax.axis_index("tm")
    place = lax.rem(position, MEM)
    group = lax.div(position, MEM)
    started = [mem_ref[k, 0, pl.ds(96, 16), :].astype(F32)[8:16] for k in range(MEM)]
    ages = [lax.rem(place - k - 1 + 2 * MEM, MEM) for k in range(MEM)]
    own_start = start_ref[0].astype(F32)
    row = lax.broadcasted_iota(jnp.int32, (SLOT, TILE), 0)
    peaks = [None] * tiles
    for k in range(MEM):
        absent = jnp.where((group == 0) & (place <= k), 1.0, 0.0) + own_start
        blocked = jnp.full((8, TILE), absent, F32)
        for other in range(MEM):
            if other != k:
                blocked = blocked + started[other] * jnp.where(ages[other] < ages[k], 1.0, 0.0)
        mk_ref[pl.ds(k * SLOT, SLOT), :] = mem_ref[k, 0]
        mv_ref[pl.ds(k * SLOT, SLOT), :] = mem_ref[k, 1]
        scores = dot_cols(mem_ref[k, 0], qs_ref[...])
        keep = (jnp.concatenate([blocked] * (SLOT // 8), axis=0) == 0.0) & (row < pooled)
        for t in range(tiles):
            piece = jnp.where(keep, scores[:, t * TILE : (t + 1) * TILE], -1e30)
            s_ref[pl.ds(k * SLOT, SLOT), pl.ds(t * TILE, TILE)] = piece
            top = jnp.max(piece.reshape(SLOT // 8, 8, TILE), axis=0)
            peaks[t] = top if peaks[t] is None else jnp.maximum(peaks[t], top)
    for load in loads:
        load.wait()
    for t in range(tiles):
        lanes = pl.ds(t * TILE, TILE)
        own_peak = m_ref[:, lanes]
        peak = jnp.maximum(own_peak, jnp.max(peaks[t], axis=0, keepdims=True))
        total = None
        for k in range(MEM):
            rows = pl.ds(k * SLOT, SLOT)
            expo = jnp.exp(s_ref[rows, lanes] - peak)
            s_ref[rows, lanes] = expo
            part = jnp.sum(expo.reshape(SLOT // 8, 8, TILE), axis=0)
            total = part if total is None else total + part
        factor = jnp.exp(own_peak - peak)
        inverse = 1.0 / (jnp.sum(total, axis=0, keepdims=True) + l_ref[:, lanes] * factor)
        mn_ref[:, lanes] = peak
        inv_ref[:, lanes] = inverse
        for k in range(MEM):
            rows = pl.ds(k * SLOT, SLOT)
            probs = s_ref[rows, lanes] * inverse
            s_ref[rows, lanes] = probs
            p_ref[rows, lanes] = probs.astype(BF16)
        ot_ref_piece = ot_ref[:, lanes] * (factor * inverse)
        dqt_ref[:, lanes] = ot_ref_piece
    out_t = dqt_ref[...] + dot_rows(mv_ref[...], p_ref[...])
    delta = jnp.sum(out_t * dost_ref[...].astype(F32), axis=0, keepdims=True)
    delta_ref[...] = delta
    attended = unstacked(out_t, tokens)
    each = tokens // (4 * keep_ref.shape[0])
    rest = jnp.zeros((keep_ref.shape[1] - 2 * each, TILE), F32)
    pieces = []
    for part in range(2 * keep_ref.shape[0]):
        low = attended[part * each : (part + 1) * each]
        high = attended[(part + 4) * each : (part + 5) * each]
        pieces.append(jnp.concatenate([low, high, rest], axis=0))
    odd = jnp.full(pieces[0].shape, lax.rem(lax.axis_index("head"), 2), jnp.int32) == 1
    for pair in range(keep_ref.shape[0]):
        even_piece, odd_piece = pieces[2 * pair], pieces[2 * pair + 1]
        keep_ref[pair] = jnp.where(odd, odd_piece, even_piece).astype(BF16)
        give_ref[pair] = jnp.where(odd, even_piece, odd_piece).astype(BF16)
    for k in range(MEM):
        rows = pl.ds(k * SLOT, SLOT)
        grad_probs = dot(mem_ref[k, 1], dost_ref[...])
        for t in range(tiles):
            lanes = pl.ds(t * TILE, TILE)
            piece = s_ref[rows, lanes] * (grad_probs[:, t * TILE : (t + 1) * TILE] - delta_ref[:, lanes])
            ds_ref[rows, lanes] = piece.astype(BF16)
        pay_ref[k, 0] = dot(ds_ref[rows, :], qs_ref[...]).astype(BF16)
        pay_ref[k, 1] = dot(p_ref[rows, :], dos_ref[...]).astype(BF16)
    dqt_ref[...] = dot_rows(mk_ref[...], ds_ref[...])


def back_body(
    q_ref, grad_ref, k_ref, v_ref, dost_ref, m_ref, inv_ref, delta_ref, dqt_ref,
    gq_ref, own_ref,
):
    tokens = k_ref.shape[0]
    width = dost_ref.shape[1]
    qs = stacked(q_ref[...].astype(F32) * HEAD_DIM**-0.5, width).astype(BF16)
    dos = stacked(grad_ref[...].astype(F32), width).astype(BF16)
    scores = dot_cols(k_ref[...], qs)
    probs = jnp.exp(scores - m_ref[...]) * inv_ref[...]
    grad_probs = dot(v_ref[...], dost_ref[...])
    grad_scores = (probs * (grad_probs - delta_ref[...])).astype(BF16)
    own_ref[0] = dot(grad_scores, qs)
    own_ref[1] = dot(probs.astype(BF16), dos)
    grad_t = (dqt_ref[...] + dot_rows(k_ref[...], grad_scores)) * HEAD_DIM**-0.5
    gq_ref[...] = unstacked(grad_t, tokens).astype(BF16)


def sum_body(got_ref, prev_ref, own_ref):
    place = lax.rem(lax.axis_index("tm"), MEM)
    prev = jnp.zeros(own_ref.shape, F32)
    own = jnp.zeros(own_ref.shape, F32)
    for i in range(MEM):
        block = got_ref[i].astype(F32)
        share = jnp.where(i <= place, 1.0, 0.0)
        prev = prev + block * share
        own = own + block * (1.0 - share)
    prev_ref[:, :SLOT, :] = prev.astype(BF16)
    prev_ref[:, SLOT:, :] = jnp.zeros((2, TILE - SLOT, TILE), BF16)
    own_ref[...] = own


def final_body(direct_ref, near_ref, far_ref, gk_ref, gv_ref):
    tokens = gk_ref.shape[0]
    row = lax.broadcasted_iota(jnp.int32, (tokens, SLOT), 0)
    col = lax.broadcasted_iota(jnp.int32, (tokens, SLOT), 1)
    matrix = jnp.where((row >> 2) == col, 1.0 / POOL, 0.0).astype(BF16)
    for which, out_ref in enumerate((gk_ref, gv_ref)):
        total = near_ref[which] + far_ref[which].astype(F32)[:SLOT]
        high = total.astype(BF16)
        low = (total - high.astype(F32)).astype(BF16)
        spread = dot(matrix, high) + dot(matrix, low)
        out_ref[...] = (direct_ref[which] + spread).astype(BF16)


def project_body(keep_ref, near_ref, w_ref, chip_ref, mine_ref, other_ref):
    upper = lax.rem(lax.axis_index("head") >> 2, 2)
    core = lax.rem(lax.axis_index("tm"), 2)
    rows = mine_ref.shape[0]
    half = w_ref.shape[1]
    total = None
    for part in range(w_ref.shape[0]):
        att = (keep_ref[part] if part < 2 else near_ref[part - 2]).astype(F32)
        swap = jnp.full(att.shape, core, jnp.int32) == 1
        att = jnp.where(swap, pltpu.roll(att, half, 1), att).astype(BF16)
        term = dot(att[:, :half], w_ref[part]) + dot(att[:, half:], chip_ref[part])
        total = term if total is None else total + term
    first, second = total[:rows], total[rows : 2 * rows]
    take = jnp.full(first.shape, upper, jnp.int32) == 1
    mine_ref[...] = jnp.where(take, second, first)
    other_ref[...] = jnp.where(take, first, second).astype(BF16)


def local(queries, key_tokens, value_tokens, out_weight, out_grad, clip_starts):
    q, k, v, grad = queries[0], key_tokens[0], value_tokens[0], out_grad[0]
    tokens = q.shape[0]
    clips = lax.axis_size("tm")
    heads = lax.axis_size("head")
    model = out_weight.shape[1]
    width = 7 * TILE
    groups = [list(range(s, s + MEM)) for s in range(0, clips, MEM)]
    me = lax.axis_index("head")
    core = lax.axis_index("tm") % 2
    half = out_weight.shape[0] // 2
    w_half = lax.dynamic_slice_in_dim(out_weight, core * half, half, 0)
    by_one, by_two, by_four = ([(h, h ^ step) for h in range(heads)] for step in (1, 2, 4))

    (own,) = call(
        pool_body, [((2, SLOT, TILE), BF16)], 10**7, 10**6, 2, 1,
        [pltpu.VMEM(k.shape, BF16), pltpu.VMEM(v.shape, BF16), pltpu.SemaphoreType.DMA((2,))],
        [pltpu.HBM] * 2, 60 * 1024 * 1024,
    )(clip_starts, k, v)
    prev = lax.ppermute(own, "tm", [(c, c + MEM) for c in range(clips - MEM)])
    grad, _ = lax.optimization_barrier((grad, own))
    grad_rows, dost = call(
        prepare_body, [((tokens, TILE), BF16), ((TILE, width), BF16)], 10**9, 2 * 10**6, 2
    )(grad, out_weight)
    w_one = lax.ppermute(w_half, "head", by_one)
    prev, grad_rows, w_one = lax.optimization_barrier((prev, grad_rows, w_one))
    w_pair = jnp.stack([w_half, w_one])
    (outgoing,) = call(choose_body, [((MEM, 2, SLOT, TILE), BF16)], 10**6, 10**6, 2)(own, prev)
    memory = lax.all_to_all(outgoing, "tm", 0, 0, axis_index_groups=groups)
    q_now, _ = lax.optimization_barrier((q, outgoing))
    m_own, l_own, ot_own = call(
        own_body, [((1, width), F32), ((1, width), F32), ((TILE, width), F32)], 10**9, 10**6, 3
    )(q_now, k, v)
    w_sent, m_own = lax.optimization_barrier((w_pair, m_own))
    w_two = lax.ppermute(w_sent, "head", by_two)
    payload, a_keep, a_give, m_all, inverse, delta, dqt = call(
        memory_body,
        [
            ((MEM, 2, SLOT, TILE), BF16), ((2, SLOT, TILE), BF16), ((2, SLOT, TILE), BF16),
            ((1, width), F32), ((1, width), F32), ((1, width), F32), ((TILE, width), F32),
        ],
        4 * 10**9, 4 * 10**6, 7, 1,
        [
            pltpu.VMEM((MEM * SLOT, width), F32), pltpu.VMEM((MEM * SLOT, width), BF16),
            pltpu.VMEM((MEM * SLOT, width), BF16), pltpu.VMEM((MEM * SLOT, TILE), BF16),
            pltpu.VMEM((MEM * SLOT, TILE), BF16), pltpu.VMEM((width, TILE), BF16),
            pltpu.VMEM((width, TILE), BF16), pltpu.VMEM((TILE, width), BF16),
            pltpu.VMEM((TILE, width), F32), pltpu.SemaphoreType.DMA((2,)),
        ],
        [pltpu.VMEM] * 5 + [pltpu.HBM] * 2,
    )(clip_starts, q, grad_rows, memory, m_own, l_own, dost, ot_own)
    arrived = lax.all_to_all(payload, "tm", 0, 0, axis_index_groups=groups)
    a_one = lax.ppermute(a_give, "head", by_one)
    w_pair, w_two, _ = lax.optimization_barrier((w_pair, w_two, a_keep))
    w_four = jnp.concatenate([w_pair, w_two])
    w_chip = lax.ppermute(w_four, "tm", [(c, c ^ 1) for c in range(clips)])
    back, near = call(
        sum_body, [((2, TILE, TILE), BF16), ((2, SLOT, TILE), F32)], 10**6, 10**6, 1
    )(arrived)
    far = lax.ppermute(back, "tm", [(c + MEM, c) for c in range(clips - MEM)])
    dost_now, _ = lax.optimization_barrier((dost, back))
    gq, direct = call(
        back_body, [((tokens, TILE), BF16), ((2, tokens, TILE), F32)], 2 * 10**9, 2 * 10**6, 9
    )(q, grad_rows, k, v, dost_now, m_all, inverse, delta, dqt)
    low = (me >> 1) & 1
    a_pair = jnp.stack([a_keep, a_one])
    a_stay = lax.dynamic_slice_in_dim(a_pair, low, 1, 1)[:, 0]
    a_send = lax.dynamic_slice_in_dim(a_pair, 1 - low, 1, 1)[:, 0]
    a_two = lax.ppermute(a_send, "head", by_two)
    a_two, _ = lax.optimization_barrier((a_two, back))
    mine, other = call(
        project_body, [((tokens // heads, model), F32), ((tokens // heads, model), BF16)], 10**4, 10**4, 4
    )(a_stay, a_two, w_four, w_chip)
    theirs = lax.ppermute(other, "head", by_four)
    projected = (mine + theirs.astype(F32)).astype(BF16)
    gk, gv = call(
        final_body, [((tokens, TILE), BF16), ((tokens, TILE), BF16)], 4 * 10**10, 10**6, 3
    )(direct, near, far)
    return projected[None], gq[None], gk[None], gv[None]


def solution(mesh):
    return jax.shard_map(
        local,
        mesh=mesh,
        in_specs=(
            P("tm", None, "head"),
            P("tm", None, "head"),
            P("tm", None, "head"),
            P("head", None),
            P("tm", None, None),
            P("tm"),
        ),
        out_specs=(
            P("tm", "head", None),
            P("tm", None, "head"),
            P("tm", None, "head"),
            P("tm", None, "head"),
        ),
        check_vma=False,
    )
```

time: 103 us -> 97.4 us (0.946)
  the two profiles are of different devices: /device:TPU:12 before, /device:TPU:26 now
where the time goes in v2:
time: 97.4 us; the launch traced here: 96.7 us
  starting transfers between devices  58 us (60%)
  waiting for transfers between devices  20 us (21%)
  Pallas kernels  13.4 us (14%)
  local copies, waits for them, and re-layouts  3.09 us (3%)
  between operations  1.49 us (2%)
    ppermute x1, starting transfers between devices, local(): prev = lax.ppermute(own, 'tm', [(c, c + MEM) for c in range(clips - MEM)])  14.8 us
    ppermute x1, waiting for transfers between devices, local(): theirs = lax.ppermute(other, 'head', by_four)  13.7 us
    ppermute x1, starting transfers between devices, local(): far = lax.ppermute(back, 'tm', [(c + MEM, c) for c in range(clips - MEM)])  13.7 us
    pallas_call x1, Pallas kernels, local(): call(memory_body, [((MEM, 2, SLOT, TILE), BF16), ((2, SLOT, TILE), BF16),...  5.62 us
    ppermute x1, starting transfers between devices, local(): a_one = lax.ppermute(a_give, 'head', by_one)  5.31 us
    all_to_all x1, starting transfers between devices, local(): memory = lax.all_to_all(outgoing, 'tm', 0, 0, axis_index_groups=groups)  4.96 us
    all_to_all x1, starting transfers between devices, local(): arrived = lax.all_to_all(payload, 'tm', 0, 0, axis_index_groups=groups)  4.86 us
    ppermute x1, starting transfers between devices, local(): w_one = lax.ppermute(w_half, 'head', by_one)  3.83 us
  transfers between devices with their start and end apart: 10, of which 4 were waited for; matrix products, arithmetic and copies ran while one was open for 0% of the time, Pallas kernels for 13%

profile of v2, /device:TPU:26, one launch (start us, length us, event | category | flops | bytes accessed | tf_op | source)
XLA Modules:
  0.0 96.7 jit_solution(3394798012090832398)
XLA Ops:
  0.7 1.0 %constant_dynamic-slice_fusion = bf16[64,1024]{1,0:T(8,128)(2,1)S(1)} fusion(bf16[128,1024]{1,0:T(8,128)(2,1)} %w_ref.1, s32[]{:T(128)S(6)} %select_n.17), kind=kLoop, calls=%fused_computation.13 | loop fusion | bytes 262148 | tf_op jit(solution)/shard_map/dynamic_slice | solution.py:274
  1.6 3.8 %collective-permute-start.1 = (bf16[64,1024]{1,0:T(8,128)(2,1)S(1)}, bf16[64,1024]{1,0:T(8,128)(2,1)S(1)}, u32[]{:S(2)}, u32[]{:S(2)}) collective-permute-start(bf16[64,1024]{1,0:T(8,128)(2,1)S(1)} %constant_dynamic-slice_fusion), channel_id=1, source_target_pairs={{0,1},{1,0},{2,3},{3,2},{4,5},{5,4},{6,7},{7,6},{8,9},{9,8},{10,11... | collective-permute-start | bytes 393224 | tf_op jit(solution)/shard_map/ppermute | solution.py:287
  6.1 1.8 %shard_map.93.own_ref = bf16[2,112,128]{2,1,0:T(8,128)(2,1)} custom-call(s32[1]{0:T(128)S(6)} %copy.11.start_ref, bf16[392,128]{1,0:T(8,128)(2,1)} %bitcast.18, bf16[392,128]{1,0:T(8,128)(2,1)} %bitcast.21), custom_call_target="tpu_custom_call" | custom-call | flops 10000000 | bytes 1000000 | tf_op jit(solution)/shard_map/pallas_call | solution.py:277
  7.9 14.8 %collective-permute-start = (bf16[2,112,128]{2,1,0:T(8,128)(2,1)}, bf16[2,112,128]{2,1,0:T(8,128)(2,1)S(1)}, u32[]{:S(2)}, u32[]{:S(2)}) collective-permute-start(bf16[2,112,128]{2,1,0:T(8,128)(2,1)} %shard_map.93.own_ref), channel_id=1, source_target_pairs={{0,64},{8,72},{16,80},{24,88},{32,96},{40,104},{48,112},{56,120},{... | collective-permute-start | bytes 172040 | tf_op jit(solution)/shard_map/ppermute | solution.py:282
  22.8 0.0 copy-start.4
  22.8 1.1 %copy-done.4 = bf16[1,392,1024]{2,1,0:T(8,128)(2,1)S(1)} copy-done((bf16[1,392,1024]{2,1,0:T(8,128)(2,1)S(1)}, bf16[1,392,1024]{2,1,0:T(8,128)(2,1)}, u32[]{:S(2)}) %copy-start.4) | copy-done | bytes 802840
  23.9 0.5 shard_map.94
  24.4 1.2 %collective-permute-done.prev_ref = bf16[2,112,128]{2,1,0:T(8,128)(2,1)S(1)} collective-permute-done((bf16[2,112,128]{2,1,0:T(8,128)(2,1)}, bf16[2,112,128]{2,1,0:T(8,128)(2,1)S(1)}, u32[]{:S(2)}, u32[]{:S(2)}) %collective-permute-start) | collective-permute-done | bytes 57376 | tf_op jit(solution)/shard_map/ppermute | solution.py:282
  25.6 0.8 shard_map.95
  26.4 5.0 %all-to-all-start = ((bf16[8,2,112,128]{3,2,1,0:T(8,128)(2,1)}), bf16[8,2,112,128]{3,2,1,0:T(8,128)(2,1)S(1)}, u32[]{:S(2)}, u32[]{:S(2)}) async-start(bf16[8,2,112,128]{3,2,1,0:T(8,128)(2,1)} %shard_map.95), calls=%async_computation | async-start | bytes 917504 | tf_op jit(solution)/shard_map/all_to_all | solution.py:291
  31.4 0.9 copy-done.2
  32.3 0.0 copy-done.3
  32.3 0.8 shard_map.96
  33.1 3.7 %collective-permute-start.4 = (bf16[2,64,1024]{2,1,0:T(8,128)(2,1)S(1)}, bf16[2,64,1024]{2,1,0:T(8,128)(2,1)S(1)}, u32[]{:S(2)}, u32[]{:S(2)}) collective-permute-start(bf16[2,64,1024]{2,1,0:T(8,128)(2,1)S(1)} %pad_maximum_fusion), channel_id=1, source_target_pairs={{0,2},{1,3},{2,0},{3,1},{4,6},{5,7},{6,4},{7,5},{8,10},{9,11},{10,... | collective-permute-start | bytes 786440 | tf_op jit(solution)/shard_map/ppermute | solution.py:297
  36.8 2.7 %all-to-all-done.mem_ref = bf16[8,2,112,128]{3,2,1,0:T(8,128)(2,1)S(1)} async-done(((bf16[8,2,112,128]{3,2,1,0:T(8,128)(2,1)}), bf16[8,2,112,128]{3,2,1,0:T(8,128)(2,1)S(1)}, u32[]{:S(2)}, u32[]{:S(2)}) %all-to-all-start) | async-done | bytes 458784 | tf_op jit(solution)/shard_map/all_to_all | solution.py:291
  39.6 5.6 %shard_map.97 = (bf16[8,2,112,128]{3,2,1,0:T(8,128)(2,1)}, bf16[2,112,128]{2,1,0:T(8,128)(2,1)S(1)}, bf16[2,112,128]{2,1,0:T(8,128)(2,1)S(1)}, f32[1,896]{1,0:T(...) custom-call(s32[1]{0:T(128)S(6)} %copy.11.start_ref, ...), custom_call_target="tpu_custom_call" | custom-call | flops 4000000000 | bytes 4000000 | tf_op jit(solution)/shard_map/pallas_call | solution.py:298
  45.2 4.9 %all-to-all-start.1 = ((bf16[8,2,112,128]{3,2,1,0:T(8,128)(2,1)}), bf16[8,2,112,128]{3,2,1,0:T(8,128)(2,1)S(1)}, u32[]{:S(2)}, u32[]{:S(2)}) async-start(bf16[8,2,112,128]{3,2,1,0:T(8,128)(2,1)} %get-tuple-element.48), calls=%async_computation.1 | async-start | bytes 917504 | tf_op jit(solution)/shard_map/all_to_all | solution.py:314
  50.1 0.0 collective-permute-done.4
  50.1 2.1 %collective-permute-start.5 = (bf16[4,64,1024]{2,1,0:T(8,128)(2,1)S(1)}, bf16[4,64,1024]{2,1,0:T(8,128)(2,1)S(1)}, u32[]{:S(2)}, u32[]{:S(2)}) collective-permute-start(bf16[4,64,1024]{2,1,0:T(8,128)(2,1)S(1)} %constant_dynamic-update-slice_fusion.w_ref), channel_id=1, source_target_pairs={{0,8},{8,0},{16,24},{24,16},{32,40},{40,32},{48,56},{56,48},{64,72... | collective-permute-start | bytes 1572872 | tf_op jit(solution)/shard_map/ppermute | solution.py:318
  52.2 5.3 %collective-permute-start.2 = (bf16[2,112,128]{2,1,0:T(8,128)(2,1)S(1)}, bf16[2,112,128]{2,1,0:T(8,128)(2,1)S(1)}, u32[]{:S(2)}, u32[]{:S(2)}) collective-permute-start(bf16[2,112,128]{2,1,0:T(8,128)(2,1)S(1)} %get-tuple-element.47), channel_id=1, source_target_pairs={{0,1},{1,0},{2,3},{3,2},{4,5},{5,4},{6,7},{7,6},{8,9},{9,8},{10,11... | collective-permute-start | bytes 172040 | tf_op jit(solution)/shard_map/ppermute | solution.py:315
  57.5 2.4 %collective-permute-done.2 = bf16[2,112,128]{2,1,0:T(8,128)(2,1)S(1)} collective-permute-done((bf16[2,112,128]{2,1,0:T(8,128)(2,1)S(1)}, bf16[2,112,128]{2,1,0:T(8,128)(2,1)S(1)}, u32[]{:S(2)}, u32[]{:S(2)}) %collective-permute-start.2) | collective-permute-done | bytes 57376 | tf_op jit(solution)/shard_map/ppermute | solution.py:315
  59.9 2.1 %collective-permute-start.3 = (bf16[2,112,128]{2,1,0:T(8,128)(2,1)S(1)}, bf16[2,112,128]{2,1,0:T(8,128)(2,1)S(1)}, u32[]{:S(2)}, u32[]{:S(2)}) collective-permute-start(bf16[2,112,128]{2,1,0:T(8,128)(2,1)S(1)} %get-tuple-element.66), channel_id=1, source_target_pairs={{0,2},{1,3},{2,0},{3,1},{4,6},{5,7},{6,4},{7,5},{8,10},{9,11},{10,... | collective-permute-start | bytes 172040 | tf_op jit(solution)/shard_map/ppermute | solution.py:331
  62.0 0.0 all-to-all-done.1.got_ref
  62.0 0.2 shard_map.98
  62.2 13.7 %collective-permute-start.7 = (bf16[2,128,128]{2,1,0:T(8,128)(2,1)S(1)}, bf16[2,128,128]{2,1,0:T(8,128)(2,1)S(1)}, u32[]{:S(2)}, u32[]{:S(2)}) collective-permute-start(bf16[2,128,128]{2,1,0:T(8,128)(2,1)S(1)} %get-tuple-element.49), channel_id=1, source_target_pairs={{64,0},{72,8},{80,16},{88,24},{96,32},{104,40},{112,48},{120,56},{... | collective-permute-start | bytes 196616 | tf_op jit(solution)/shard_map/ppermute | solution.py:322
  75.9 1.9 %shard_map.100 = (bf16[392,128]{1,0:T(8,128)(2,1)}, f32[2,392,128]{2,1,0:T(8,128)S(1)}) custom-call(bf16[392,128]{1,0:T(8,128)(2,1)S(1)} %bitcast.28, bf16[392,128]{1,0:T(8,128)(2,1)S(1)} %get-tuple-element.37.grad_ref, bf16[392,128]{1,0:T(8,128)(2,1)S(1)} %bitcast.20, bf16[392,128]{1,0:T(8,128)(2,1)S(1)} %bitcast.23, ...), custom_call_target="tpu_custom_call" | custom-call | flops 2000000000 | bytes 2000000 | tf_op jit(solution)/shard_map/pallas_call | solution.py:324
  77.8 0.0 collective-permute-done.3.near_ref
  77.8 0.8 shard_map.99
  78.6 2.7 %collective-permute-start.6 = (bf16[49,1024]{1,0:T(8,128)(2,1)S(1)}, bf16[49,1024]{1,0:T(8,128)(2,1)S(1)}, u32[]{:S(2)}, u32[]{:S(2)}) collective-permute-start(bf16[49,1024]{1,0:T(8,128)(2,1)S(1)} %get-tuple-element.55), channel_id=1, source_target_pairs={{0,4},{1,5},{2,6},{3,7},{4,0},{5,1},{6,2},{7,3},{8,12},{9,13},{10,... | collective-permute-start | bytes 301064 | tf_op jit(solution)/shard_map/ppermute | solution.py:336
  81.3 1.0 %shard_map.101 = (bf16[392,128]{1,0:T(8,128)(2,1)}, bf16[392,128]{1,0:T(8,128)(2,1)}) custom-call(f32[2,392,128]{2,1,0:T(8,128)S(1)} %get-tuple-element.62.direct_ref, f32[2,112,128]{2,1,0:T(8,128)S(1)} %get-tuple-element.63.near_ref, bf16[2,128,128]{2,1,0:T(8,128)(2,1)S(1)} %collective-permute-done.7.far_ref), custom_call_target="tpu_custom_call" | custom-call | flops 40000000000 | bytes 1000000 | tf_op jit(solution)/shard_map/pallas_call | solution.py:338
  82.3 13.7 %collective-permute-done.6 = bf16[49,1024]{1,0:T(8,128)(2,1)S(1)} collective-permute-done((bf16[49,1024]{1,0:T(8,128)(2,1)S(1)}, bf16[49,1024]{1,0:T(8,128)(2,1)S(1)}, u32[]{:S(2)}, u32[]{:S(2)}) %collective-permute-start.6) | collective-permute-done | bytes 100384 | tf_op jit(solution)/shard_map/ppermute | solution.py:336
  96.0 0.7 fusion
  (16 shorter events, 0.1 us)
Async XLA Ops:
  0.6 22.1 %copy-start = (bf16[128,1024]{1,0:T(8,128)(2,1)S(1)}, bf16[128,1024]{1,0:T(8,128)(2,1)}, u32[]{:S(2)}) copy-start(bf16[128,1024]{1,0:T(8,128)(2,1)} %w_ref.1) | copy-start | bytes 786436
  1.6 23.9 %collective-permute-start.1 = (bf16[64,1024]{1,0:T(8,128)(2,1)S(1)}, bf16[64,1024]{1,0:T(8,128)(2,1)S(1)}, u32[]{:S(2)}, u32[]{:S(2)}) collective-permute-start(bf16[64,1024]{1,0:T(8,128)(2,1)S(1)} %constant_dynamic-slice_fusion), channel_id=1, source_target_pairs={{0,1},{1,0},{2,3},{3,2},{4,5},{5,4},{6,7},{7,6},{8,9},{9,8},{10,11... | collective-permute-start | bytes 393224 | tf_op jit(solution)/shard_map/ppermute | solution.py:287
  7.9 17.7 %collective-permute-start = (bf16[2,112,128]{2,1,0:T(8,128)(2,1)}, bf16[2,112,128]{2,1,0:T(8,128)(2,1)S(1)}, u32[]{:S(2)}, u32[]{:S(2)}) collective-permute-start(bf16[2,112,128]{2,1,0:T(8,128)(2,1)} %shard_map.93.own_ref), channel_id=1, source_target_pairs={{0,64},{8,72},{16,80},{24,88},{32,96},{40,104},{48,112},{56,120},{... | collective-permute-start | bytes 172040 | tf_op jit(solution)/shard_map/ppermute | solution.py:282
  22.8 1.1 %copy-start.4 = (bf16[1,392,1024]{2,1,0:T(8,128)(2,1)S(1)}, bf16[1,392,1024]{2,1,0:T(8,128)(2,1)}, u32[]{:S(2)}) copy-start(bf16[1,392,1024]{2,1,0:T(8,128)(2,1)} %param.10) | copy-start | bytes 2408452
  23.9 1.7 %copy-start.1 = (bf16[2,112,128]{2,1,0:T(8,128)(2,1)S(1)}, bf16[2,112,128]{2,1,0:T(8,128)(2,1)}, u32[]{:S(2)}) copy-start(bf16[2,112,128]{2,1,0:T(8,128)(2,1)} %shard_map.93.own_ref) | copy-start | bytes 172036
  26.4 5.0 %copy-start.5 = (bf16[1,392,128]{2,1,0:T(8,128)(2,1)S(1)}, bf16[1,392,128]{2,1,0:T(8,128)(2,1)}, u32[]{:S(2)}) copy-start(bf16[1,392,128]{2,1,0:T(8,128)(2,1)} %param.6) | copy-start | bytes 301060
  26.4 13.2 %all-to-all-start = ((bf16[8,2,112,128]{3,2,1,0:T(8,128)(2,1)}), bf16[8,2,112,128]{3,2,1,0:T(8,128)(2,1)S(1)}, u32[]{:S(2)}, u32[]{:S(2)}) async-start(bf16[8,2,112,128]{3,2,1,0:T(8,128)(2,1)} %shard_map.95), calls=%async_computation | async-start | bytes 917504 | tf_op jit(solution)/shard_map/all_to_all | solution.py:291
  31.4 0.9 copy-start.2
  31.4 0.9 copy-start.3
  33.1 16.9 %collective-permute-start.4 = (bf16[2,64,1024]{2,1,0:T(8,128)(2,1)S(1)}, bf16[2,64,1024]{2,1,0:T(8,128)(2,1)S(1)}, u32[]{:S(2)}, u32[]{:S(2)}) collective-permute-start(bf16[2,64,1024]{2,1,0:T(8,128)(2,1)S(1)} %pad_maximum_fusion), channel_id=1, source_target_pairs={{0,2},{1,3},{2,0},{3,1},{4,6},{5,7},{6,4},{7,5},{8,10},{9,11},{10,... | collective-permute-start | bytes 786440 | tf_op jit(solution)/shard_map/ppermute | solution.py:297
  45.2 16.8 %all-to-all-start.1 = ((bf16[8,2,112,128]{3,2,1,0:T(8,128)(2,1)}), bf16[8,2,112,128]{3,2,1,0:T(8,128)(2,1)S(1)}, u32[]{:S(2)}, u32[]{:S(2)}) async-start(bf16[8,2,112,128]{3,2,1,0:T(8,128)(2,1)} %get-tuple-element.48), calls=%async_computation.1 | async-start | bytes 917504 | tf_op jit(solution)/shard_map/all_to_all | solution.py:314
  50.1 27.7 %collective-permute-start.5 = (bf16[4,64,1024]{2,1,0:T(8,128)(2,1)S(1)}, bf16[4,64,1024]{2,1,0:T(8,128)(2,1)S(1)}, u32[]{:S(2)}, u32[]{:S(2)}) collective-permute-start(bf16[4,64,1024]{2,1,0:T(8,128)(2,1)S(1)} %constant_dynamic-update-slice_fusion.w_ref), channel_id=1, source_target_pairs={{0,8},{8,0},{16,24},{24,16},{32,40},{40,32},{48,56},{56,48},{64,72... | collective-permute-start | bytes 1572872 | tf_op jit(solution)/shard_map/ppermute | solution.py:318
  52.2 7.7 %collective-permute-start.2 = (bf16[2,112,128]{2,1,0:T(8,128)(2,1)S(1)}, bf16[2,112,128]{2,1,0:T(8,128)(2,1)S(1)}, u32[]{:S(2)}, u32[]{:S(2)}) collective-permute-start(bf16[2,112,128]{2,1,0:T(8,128)(2,1)S(1)} %get-tuple-element.47), channel_id=1, source_target_pairs={{0,1},{1,0},{2,3},{3,2},{4,5},{5,4},{6,7},{7,6},{8,9},{9,8},{10,11... | collective-permute-start | bytes 172040 | tf_op jit(solution)/shard_map/ppermute | solution.py:315
  59.9 17.9 %collective-permute-start.3 = (bf16[2,112,128]{2,1,0:T(8,128)(2,1)S(1)}, bf16[2,112,128]{2,1,0:T(8,128)(2,1)S(1)}, u32[]{:S(2)}, u32[]{:S(2)}) collective-permute-start(bf16[2,112,128]{2,1,0:T(8,128)(2,1)S(1)} %get-tuple-element.66), channel_id=1, source_target_pairs={{0,2},{1,3},{2,0},{3,1},{4,6},{5,7},{6,4},{7,5},{8,10},{9,11},{10,... | collective-permute-start | bytes 172040 | tf_op jit(solution)/shard_map/ppermute | solution.py:331
  62.2 19.1 %collective-permute-start.7 = (bf16[2,128,128]{2,1,0:T(8,128)(2,1)S(1)}, bf16[2,128,128]{2,1,0:T(8,128)(2,1)S(1)}, u32[]{:S(2)}, u32[]{:S(2)}) collective-permute-start(bf16[2,128,128]{2,1,0:T(8,128)(2,1)S(1)} %get-tuple-element.49), channel_id=1, source_target_pairs={{64,0},{72,8},{80,16},{88,24},{96,32},{104,40},{112,48},{120,56},{... | collective-permute-start | bytes 196616 | tf_op jit(solution)/shard_map/ppermute | solution.py:322
  78.6 17.5 %collective-permute-start.6 = (bf16[49,1024]{1,0:T(8,128)(2,1)S(1)}, bf16[49,1024]{1,0:T(8,128)(2,1)S(1)}, u32[]{:S(2)}, u32[]{:S(2)}) collective-permute-start(bf16[49,1024]{1,0:T(8,128)(2,1)S(1)} %get-tuple-element.55), channel_id=1, source_target_pairs={{0,4},{1,5},{2,6},{3,7},{4,0},{5,1},{6,2},{7,3},{8,12},{9,13},{10,... | collective-permute-start | bytes 301064 | tf_op jit(solution)/shard_map/ppermute | solution.py:336

commit v3 on v2

--- a/solution.py
+++ b/solution.py
@@ -271,7 +271,6 @@
     me = lax.axis_index("head")
     core = lax.axis_index("tm") % 2
     half = out_weight.shape[0] // 2
-    w_half = lax.dynamic_slice_in_dim(out_weight, core * half, half, 0)
     by_one, by_two, by_four = ([(h, h ^ step) for h in range(heads)] for step in (1, 2, 4))
 
     (own,) = call(
@@ -284,10 +283,13 @@
     grad_rows, dost = call(
         prepare_body, [((tokens, TILE), BF16), ((TILE, width), BF16)], 10**9, 2 * 10**6, 2
     )(grad, out_weight)
+    w_seen, _ = lax.optimization_barrier((out_weight, own))
+    w_half = lax.dynamic_slice_in_dim(w_seen, core * half, half, 0)
     w_one = lax.ppermute(w_half, "head", by_one)
-    prev, grad_rows, w_one = lax.optimization_barrier((prev, grad_rows, w_one))
+    prev, grad_rows = lax.optimization_barrier((prev, grad_rows))
+    (outgoing,) = call(choose_body, [((MEM, 2, SLOT, TILE), BF16)], 2 * 10**10, 10**6, 2)(own, prev)
+    outgoing, w_one = lax.optimization_barrier((outgoing, w_one))
     w_pair = jnp.stack([w_half, w_one])
-    (outgoing,) = call(choose_body, [((MEM, 2, SLOT, TILE), BF16)], 10**6, 10**6, 2)(own, prev)
     memory = lax.all_to_all(outgoing, "tm", 0, 0, axis_index_groups=groups)
     q_now, _ = lax.optimization_barrier((q, outgoing))
     m_own, l_own, ot_own = call(
@@ -317,12 +319,11 @@
     w_four = jnp.concatenate([w_pair, w_two])
     w_chip = lax.ppermute(w_four, "tm", [(c, c ^ 1) for c in range(clips)])
     back, near = call(
-        sum_body, [((2, TILE, TILE), BF16), ((2, SLOT, TILE), F32)], 10**6, 10**6, 1
+        sum_body, [((2, TILE, TILE), BF16), ((2, SLOT, TILE), F32)], 2 * 10**10, 10**6, 1
     )(arrived)
-    far = lax.ppermute(back, "tm", [(c + MEM, c) for c in range(clips - MEM)])
     dost_now, _ = lax.optimization_barrier((dost, back))
     gq, direct = call(
-        back_body, [((tokens, TILE), BF16), ((2, tokens, TILE), F32)], 2 * 10**9, 2 * 10**6, 9
+        back_body, [((tokens, TILE), BF16), ((2, tokens, TILE), F32)], 10**4, 10**4, 9
     )(q, grad_rows, k, v, dost_now, m_all, inverse, delta, dqt)
     low = (me >> 1) & 1
     a_pair = jnp.stack([a_keep, a_one])
@@ -333,10 +334,12 @@
     mine, other = call(
         project_body, [((tokens // heads, model), F32), ((tokens // heads, model), BF16)], 10**4, 10**4, 4
     )(a_stay, a_two, w_four, w_chip)
+    back, mine = lax.optimization_barrier((back, mine))
+    far = lax.ppermute(back, "tm", [(c + MEM, c) for c in range(clips - MEM)])
     theirs = lax.ppermute(other, "head", by_four)
     projected = (mine + theirs.astype(F32)).astype(BF16)
     gk, gv = call(
-        final_body, [((tokens, TILE), BF16), ((tokens, TILE), BF16)], 4 * 10**10, 10**6, 3
+        final_body, [((tokens, TILE), BF16), ((tokens, TILE), BF16)], 10**4, 10**4, 3
     )(direct, near, far)
     return projected[None], gq[None], gk[None], gv[None]
 

time: 97.4 us -> 93.1 us (0.956)
  the two profiles are of different devices: /device:TPU:26 before, /device:TPU:122 now
where the time goes in v3:
time: 93.1 us; the launch traced here: 92.5 us
  starting transfers between devices  53.8 us (58%)
  waiting for transfers between devices  20.7 us (22%)
  Pallas kernels  13.4 us (14%)
  local copies, waits for them, and re-layouts  2.42 us (3%)
  between operations  1.54 us (2%)
    ppermute x1, waiting for transfers between devices, local(): far = lax.ppermute(back, 'tm', [(c + MEM, c) for c in range(clips - MEM)])  14.3 us
    ppermute x1, starting transfers between devices, local(): prev = lax.ppermute(own, 'tm', [(c, c + MEM) for c in range(clips - MEM)])  13 us
    ppermute x1, starting transfers between devices, local(): far = lax.ppermute(back, 'tm', [(c + MEM, c) for c in range(clips - MEM)])  7.04 us
    ppermute x1, starting transfers between devices, local(): theirs = lax.ppermute(other, 'head', by_four)  5.91 us
    pallas_call x1, Pallas kernels, local(): call(memory_body, [((MEM, 2, SLOT, TILE), BF16), ((2, SLOT, TILE), BF16),...  5.63 us
    all_to_all x1, starting transfers between devices, local(): memory = lax.all_to_all(outgoing, 'tm', 0, 0, axis_index_groups=groups)  4.96 us
    all_to_all x1, starting transfers between devices, local(): arrived = lax.all_to_all(payload, 'tm', 0, 0, axis_index_groups=groups)  4.86 us
    ppermute x1, starting transfers between devices, local(): a_two = lax.ppermute(a_send, 'head', by_two)  4.58 us
  transfers between devices with their start and end apart: 10, of which 5 were waited for; matrix products, arithmetic and copies ran while one was open for 0% of the time, Pallas kernels for 12%

profile of v3, /device:TPU:122, one launch (start us, length us, event | category | flops | bytes accessed | tf_op | source)
XLA Modules:
  0.0 92.5 jit_solution(2881483870948953907)
XLA Ops:
  1.3 1.8 %shard_map.93.own_ref = bf16[2,112,128]{2,1,0:T(8,128)(2,1)} custom-call(s32[1]{0:T(128)S(6)} %copy.11.start_ref, bf16[392,128]{1,0:T(8,128)(2,1)} %bitcast.18, bf16[392,128]{1,0:T(8,128)(2,1)} %bitcast.21), custom_call_target="tpu_custom_call" | custom-call | flops 10000000 | bytes 1000000 | tf_op jit(solution)/shard_map/pallas_call | solution.py:276
  3.1 13.0 %collective-permute-start = (bf16[2,112,128]{2,1,0:T(8,128)(2,1)}, bf16[2,112,128]{2,1,0:T(8,128)(2,1)S(1)}, u32[]{:S(2)}, u32[]{:S(2)}) collective-permute-start(bf16[2,112,128]{2,1,0:T(8,128)(2,1)} %shard_map.93.own_ref), channel_id=1, source_target_pairs={{0,64},{8,72},{16,80},{24,88},{32,96},{40,104},{48,112},{56,120},{... | collective-permute-start | bytes 172040 | tf_op jit(solution)/shard_map/ppermute | solution.py:281
  16.2 2.9 %collective-permute-start.1 = (bf16[64,1024]{1,0:T(8,128)(2,1)S(1)}, bf16[64,1024]{1,0:T(8,128)(2,1)S(1)}, u32[]{:S(2)}, u32[]{:S(2)}) collective-permute-start(bf16[64,1024]{1,0:T(8,128)(2,1)S(1)} %constant_dynamic-slice_fusion), channel_id=1, source_target_pairs={{0,1},{1,0},{2,3},{3,2},{4,5},{5,4},{6,7},{7,6},{8,9},{9,8},{10,11... | collective-permute-start | bytes 393224 | tf_op jit(solution)/shard_map/ppermute | solution.py:288
  19.1 0.0 copy-start.5
  19.2 1.1 %copy-done.5 = bf16[1,392,1024]{2,1,0:T(8,128)(2,1)S(1)} copy-done((bf16[1,392,1024]{2,1,0:T(8,128)(2,1)S(1)}, bf16[1,392,1024]{2,1,0:T(8,128)(2,1)}, u32[]{:S(2)}) %copy-start.5) | copy-done | bytes 802840
  20.3 0.5 shard_map.94
  20.8 0.3 copy-done.4
  21.1 0.8 shard_map.95
  21.9 1.4 %collective-permute-done.1 = bf16[64,1024]{1,0:T(8,128)(2,1)S(1)} collective-permute-done((bf16[64,1024]{1,0:T(8,128)(2,1)S(1)}, bf16[64,1024]{1,0:T(8,128)(2,1)S(1)}, u32[]{:S(2)}, u32[]{:S(2)}) %collective-permute-start.1) | collective-permute-done | bytes 131104 | tf_op jit(solution)/shard_map/ppermute | solution.py:288
  23.3 5.0 %all-to-all-start = ((bf16[8,2,112,128]{3,2,1,0:T(8,128)(2,1)}), bf16[8,2,112,128]{3,2,1,0:T(8,128)(2,1)S(1)}, u32[]{:S(2)}, u32[]{:S(2)}) async-start(bf16[8,2,112,128]{3,2,1,0:T(8,128)(2,1)} %shard_map.95), calls=%async_computation | async-start | bytes 917504 | tf_op jit(solution)/shard_map/all_to_all | solution.py:293
  28.3 0.9 copy-done
  29.2 0.0 copy-done.1
  29.2 0.8 shard_map.96
  30.0 4.4 %collective-permute-start.4 = (bf16[2,64,1024]{2,1,0:T(8,128)(2,1)S(1)}, bf16[2,64,1024]{2,1,0:T(8,128)(2,1)S(1)}, u32[]{:S(2)}, u32[]{:S(2)}) collective-permute-start(bf16[2,64,1024]{2,1,0:T(8,128)(2,1)S(1)} %pad_maximum_fusion), channel_id=1, source_target_pairs={{0,2},{1,3},{2,0},{3,1},{4,6},{5,7},{6,4},{7,5},{8,10},{9,11},{10,... | collective-permute-start | bytes 786440 | tf_op jit(solution)/shard_map/ppermute | solution.py:299
  34.4 2.0 %all-to-all-done.mem_ref = bf16[8,2,112,128]{3,2,1,0:T(8,128)(2,1)S(1)} async-done(((bf16[8,2,112,128]{3,2,1,0:T(8,128)(2,1)}), bf16[8,2,112,128]{3,2,1,0:T(8,128)(2,1)S(1)}, u32[]{:S(2)}, u32[]{:S(2)}) %all-to-all-start) | async-done | bytes 458784 | tf_op jit(solution)/shard_map/all_to_all | solution.py:293
  36.5 5.6 %shard_map.97 = (bf16[8,2,112,128]{3,2,1,0:T(8,128)(2,1)}, bf16[2,112,128]{2,1,0:T(8,128)(2,1)S(1)}, bf16[2,112,128]{2,1,0:T(8,128)(2,1)S(1)}, f32[1,896]{1,0:T(...) custom-call(s32[1]{0:T(128)S(6)} %copy.11.start_ref, ...), custom_call_target="tpu_custom_call" | custom-call | flops 4000000000 | bytes 4000000 | tf_op jit(solution)/shard_map/pallas_call | solution.py:300
  42.1 4.9 %all-to-all-start.1 = ((bf16[8,2,112,128]{3,2,1,0:T(8,128)(2,1)}), bf16[8,2,112,128]{3,2,1,0:T(8,128)(2,1)S(1)}, u32[]{:S(2)}, u32[]{:S(2)}) async-start(bf16[8,2,112,128]{3,2,1,0:T(8,128)(2,1)} %get-tuple-element.52), calls=%async_computation.1 | async-start | bytes 917504 | tf_op jit(solution)/shard_map/all_to_all | solution.py:316
  47.0 0.0 collective-permute-done.4
  47.0 4.2 %collective-permute-start.2 = (bf16[2,112,128]{2,1,0:T(8,128)(2,1)S(1)}, bf16[2,112,128]{2,1,0:T(8,128)(2,1)S(1)}, u32[]{:S(2)}, u32[]{:S(2)}) collective-permute-start(bf16[2,112,128]{2,1,0:T(8,128)(2,1)S(1)} %get-tuple-element.55), channel_id=1, source_target_pairs={{0,1},{1,0},{2,3},{3,2},{4,5},{5,4},{6,7},{7,6},{8,9},{9,8},{10,11... | collective-permute-start | bytes 172040 | tf_op jit(solution)/shard_map/ppermute | solution.py:317
  51.2 1.9 %collective-permute-start.5 = (bf16[4,64,1024]{2,1,0:T(8,128)(2,1)S(1)}, bf16[4,64,1024]{2,1,0:T(8,128)(2,1)S(1)}, u32[]{:S(2)}, u32[]{:S(2)}) collective-permute-start(bf16[4,64,1024]{2,1,0:T(8,128)(2,1)S(1)} %constant_dynamic-update-slice_fusion.w_ref), channel_id=1, source_target_pairs={{0,8},{8,0},{16,24},{24,16},{32,40},{40,32},{48,56},{56,48},{64,72... | collective-permute-start | bytes 1572872 | tf_op jit(solution)/shard_map/ppermute | solution.py:320
  53.1 0.2 collective-permute-done.2
  53.4 4.6 %collective-permute-start.3 = (bf16[2,112,128]{2,1,0:T(8,128)(2,1)S(1)}, bf16[2,112,128]{2,1,0:T(8,128)(2,1)S(1)}, u32[]{:S(2)}, u32[]{:S(2)}) collective-permute-start(bf16[2,112,128]{2,1,0:T(8,128)(2,1)S(1)} %get-tuple-element.74), channel_id=1, source_target_pairs={{0,2},{1,3},{2,0},{3,1},{4,6},{5,7},{6,4},{7,5},{8,10},{9,11},{10,... | collective-permute-start | bytes 172040 | tf_op jit(solution)/shard_map/ppermute | solution.py:332
  58.0 0.0 all-to-all-done.1.got_ref
  58.0 0.2 shard_map.98
  58.2 2.8 %collective-permute-done.3.near_ref = bf16[2,112,128]{2,1,0:T(8,128)(2,1)S(1)} collective-permute-done((bf16[2,112,128]{2,1,0:T(8,128)(2,1)S(1)}, bf16[2,112,128]{2,1,0:T(8,128)(2,1)S(1)}, u32[]{:S(2)}, u32[]{:S(2)}) %collective-permute-start.3) | collective-permute-done | bytes 57376 | tf_op jit(solution)/shard_map/ppermute | solution.py:332
  60.9 0.8 shard_map.99
  61.7 5.9 %collective-permute-start.6 = (bf16[49,1024]{1,0:T(8,128)(2,1)S(1)}, bf16[49,1024]{1,0:T(8,128)(2,1)S(1)}, u32[]{:S(2)}, u32[]{:S(2)}) collective-permute-start(bf16[49,1024]{1,0:T(8,128)(2,1)S(1)} %get-tuple-element.62), channel_id=1, source_target_pairs={{0,4},{1,5},{2,6},{3,7},{4,0},{5,1},{6,2},{7,3},{8,12},{9,13},{10,... | collective-permute-start | bytes 301064 | tf_op jit(solution)/shard_map/ppermute | solution.py:339
  67.6 7.0 %collective-permute-start.7 = (bf16[2,128,128]{2,1,0:T(8,128)(2,1)S(1)}, bf16[2,128,128]{2,1,0:T(8,128)(2,1)S(1)}, u32[]{:S(2)}, u32[]{:S(2)}) collective-permute-start(bf16[2,128,128]{2,1,0:T(8,128)(2,1)S(1)} %get-tuple-element.71), channel_id=1, source_target_pairs={{64,0},{72,8},{80,16},{88,24},{96,32},{104,40},{112,48},{120,56},{... | collective-permute-start | bytes 196616 | tf_op jit(solution)/shard_map/ppermute | solution.py:338
  74.7 1.9 %shard_map.100 = (bf16[392,128]{1,0:T(8,128)(2,1)}, f32[2,392,128]{2,1,0:T(8,128)S(1)}) custom-call(bf16[392,128]{1,0:T(8,128)(2,1)S(1)} %bitcast.26, bf16[392,128]{1,0:T(8,128)(2,1)S(1)} %get-tuple-element.41.grad_ref, bf16[392,128]{1,0:T(8,128)(2,1)S(1)} %bitcast.20, bf16[392,128]{1,0:T(8,128)(2,1)S(1)} %bitcast.23, ...), custom_call_target="tpu_custom_call" | custom-call | flops 10000 | bytes 10000 | tf_op jit(solution)/shard_map/pallas_call | solution.py:325
  76.5 14.3 %collective-permute-done.7.far_ref = bf16[2,128,128]{2,1,0:T(8,128)(2,1)S(1)} collective-permute-done((bf16[2,128,128]{2,1,0:T(8,128)(2,1)S(1)}, bf16[2,128,128]{2,1,0:T(8,128)(2,1)S(1)}, u32[]{:S(2)}, u32[]{:S(2)}) %collective-permute-start.7) | collective-permute-done | bytes 65568 | tf_op jit(solution)/shard_map/ppermute | solution.py:338
  90.8 1.0 %shard_map.101 = (bf16[392,128]{1,0:T(8,128)(2,1)}, bf16[392,128]{1,0:T(8,128)(2,1)}) custom-call(f32[2,392,128]{2,1,0:T(8,128)S(1)} %get-tuple-element.69.direct_ref, f32[2,112,128]{2,1,0:T(8,128)S(1)} %get-tuple-element.70.near_ref, bf16[2,128,128]{2,1,0:T(8,128)(2,1)S(1)} %collective-permute-done.7.far_ref), custom_call_target="tpu_custom_call" | custom-call | flops 10000 | bytes 10000 | tf_op jit(solution)/shard_map/pallas_call | solution.py:341
  91.8 0.7 fusion
  (16 shorter events, 0.1 us)
Async XLA Ops:
  0.6 15.6 %copy-start.2 = (bf16[128,1024]{1,0:T(8,128)(2,1)S(1)}, bf16[128,1024]{1,0:T(8,128)(2,1)}, u32[]{:S(2)}) copy-start(bf16[128,1024]{1,0:T(8,128)(2,1)} %w_ref.1) | copy-start | bytes 786436
  3.1 17.7 %collective-permute-start = (bf16[2,112,128]{2,1,0:T(8,128)(2,1)}, bf16[2,112,128]{2,1,0:T(8,128)(2,1)S(1)}, u32[]{:S(2)}, u32[]{:S(2)}) collective-permute-start(bf16[2,112,128]{2,1,0:T(8,128)(2,1)} %shard_map.93.own_ref), channel_id=1, source_target_pairs={{0,64},{8,72},{16,80},{24,88},{32,96},{40,104},{48,112},{56,120},{... | collective-permute-start | bytes 172040 | tf_op jit(solution)/shard_map/ppermute | solution.py:281
  16.2 7.1 %collective-permute-start.1 = (bf16[64,1024]{1,0:T(8,128)(2,1)S(1)}, bf16[64,1024]{1,0:T(8,128)(2,1)S(1)}, u32[]{:S(2)}, u32[]{:S(2)}) collective-permute-start(bf16[64,1024]{1,0:T(8,128)(2,1)S(1)} %constant_dynamic-slice_fusion), channel_id=1, source_target_pairs={{0,1},{1,0},{2,3},{3,2},{4,5},{5,4},{6,7},{7,6},{8,9},{9,8},{10,11... | collective-permute-start | bytes 393224 | tf_op jit(solution)/shard_map/ppermute | solution.py:288
  19.1 1.1 %copy-start.5 = (bf16[1,392,1024]{2,1,0:T(8,128)(2,1)S(1)}, bf16[1,392,1024]{2,1,0:T(8,128)(2,1)}, u32[]{:S(2)}) copy-start(bf16[1,392,1024]{2,1,0:T(8,128)(2,1)} %param.10) | copy-start | bytes 2408452
  20.3 0.8 copy-start.4
  23.3 5.0 %copy-start.3 = (bf16[1,392,128]{2,1,0:T(8,128)(2,1)S(1)}, bf16[1,392,128]{2,1,0:T(8,128)(2,1)}, u32[]{:S(2)}) copy-start(bf16[1,392,128]{2,1,0:T(8,128)(2,1)} %param.6) | copy-start | bytes 301060
  23.3 13.2 %all-to-all-start = ((bf16[8,2,112,128]{3,2,1,0:T(8,128)(2,1)}), bf16[8,2,112,128]{3,2,1,0:T(8,128)(2,1)S(1)}, u32[]{:S(2)}, u32[]{:S(2)}) async-start(bf16[8,2,112,128]{3,2,1,0:T(8,128)(2,1)} %shard_map.95), calls=%async_computation | async-start | bytes 917504 | tf_op jit(solution)/shard_map/all_to_all | solution.py:293
  28.3 0.9 copy-start
  28.3 0.9 %copy-start.1 = (bf16[1,392,128]{2,1,0:T(8,128)(2,1)S(1)}, bf16[1,392,128]{2,1,0:T(8,128)(2,1)}, u32[]{:S(2)}) copy-start(bf16[1,392,128]{2,1,0:T(8,128)(2,1)} %param.8) | copy-start | bytes 301060
  30.0 16.9 %collective-permute-start.4 = (bf16[2,64,1024]{2,1,0:T(8,128)(2,1)S(1)}, bf16[2,64,1024]{2,1,0:T(8,128)(2,1)S(1)}, u32[]{:S(2)}, u32[]{:S(2)}) collective-permute-start(bf16[2,64,1024]{2,1,0:T(8,128)(2,1)S(1)} %pad_maximum_fusion), channel_id=1, source_target_pairs={{0,2},{1,3},{2,0},{3,1},{4,6},{5,7},{6,4},{7,5},{8,10},{9,11},{10,... | collective-permute-start | bytes 786440 | tf_op jit(solution)/shard_map/ppermute | solution.py:299
  42.1 15.9 %all-to-all-start.1 = ((bf16[8,2,112,128]{3,2,1,0:T(8,128)(2,1)}), bf16[8,2,112,128]{3,2,1,0:T(8,128)(2,1)S(1)}, u32[]{:S(2)}, u32[]{:S(2)}) async-start(bf16[8,2,112,128]{3,2,1,0:T(8,128)(2,1)} %get-tuple-element.52), calls=%async_computation.1 | async-start | bytes 917504 | tf_op jit(solution)/shard_map/all_to_all | solution.py:316
  47.0 6.4 %collective-permute-start.2 = (bf16[2,112,128]{2,1,0:T(8,128)(2,1)S(1)}, bf16[2,112,128]{2,1,0:T(8,128)(2,1)S(1)}, u32[]{:S(2)}, u32[]{:S(2)}) collective-permute-start(bf16[2,112,128]{2,1,0:T(8,128)(2,1)S(1)} %get-tuple-element.55), channel_id=1, source_target_pairs={{0,1},{1,0},{2,3},{3,2},{4,5},{5,4},{6,7},{7,6},{8,9},{9,8},{10,11... | collective-permute-start | bytes 172040 | tf_op jit(solution)/shard_map/ppermute | solution.py:317
  51.2 9.7 %collective-permute-start.5 = (bf16[4,64,1024]{2,1,0:T(8,128)(2,1)S(1)}, bf16[4,64,1024]{2,1,0:T(8,128)(2,1)S(1)}, u32[]{:S(2)}, u32[]{:S(2)}) collective-permute-start(bf16[4,64,1024]{2,1,0:T(8,128)(2,1)S(1)} %constant_dynamic-update-slice_fusion.w_ref), channel_id=1, source_target_pairs={{0,8},{8,0},{16,24},{24,16},{32,40},{40,32},{48,56},{56,48},{64,72... | collective-permute-start | bytes 1572872 | tf_op jit(solution)/shard_map/ppermute | solution.py:320
  53.4 7.6 %collective-permute-start.3 = (bf16[2,112,128]{2,1,0:T(8,128)(2,1)S(1)}, bf16[2,112,128]{2,1,0:T(8,128)(2,1)S(1)}, u32[]{:S(2)}, u32[]{:S(2)}) collective-permute-start(bf16[2,112,128]{2,1,0:T(8,128)(2,1)S(1)} %get-tuple-element.74), channel_id=1, source_target_pairs={{0,2},{1,3},{2,0},{3,1},{4,6},{5,7},{6,4},{7,5},{8,10},{9,11},{10,... | collective-permute-start | bytes 172040 | tf_op jit(solution)/shard_map/ppermute | solution.py:332
  61.7 30.1 %collective-permute-start.6 = (bf16[49,1024]{1,0:T(8,128)(2,1)S(1)}, bf16[49,1024]{1,0:T(8,128)(2,1)S(1)}, u32[]{:S(2)}, u32[]{:S(2)}) collective-permute-start(bf16[49,1024]{1,0:T(8,128)(2,1)S(1)} %get-tuple-element.62), channel_id=1, source_target_pairs={{0,4},{1,5},{2,6},{3,7},{4,0},{5,1},{6,2},{7,3},{8,12},{9,13},{10,... | collective-permute-start | bytes 301064 | tf_op jit(solution)/shard_map/ppermute | solution.py:339
  67.6 23.2 %collective-permute-start.7 = (bf16[2,128,128]{2,1,0:T(8,128)(2,1)S(1)}, bf16[2,128,128]{2,1,0:T(8,128)(2,1)S(1)}, u32[]{:S(2)}, u32[]{:S(2)}) collective-permute-start(bf16[2,128,128]{2,1,0:T(8,128)(2,1)S(1)} %get-tuple-element.71), channel_id=1, source_target_pairs={{64,0},{72,8},{80,16},{88,24},{96,32},{104,40},{112,48},{120,56},{... | collective-permute-start | bytes 196616 | tf_op jit(solution)/shard_map/ppermute | solution.py:338

commit v4 on v3

--- a/solution.py
+++ b/solution.py
@@ -224,8 +224,7 @@
         share = jnp.where(i <= place, 1.0, 0.0)
         prev = prev + block * share
         own = own + block * (1.0 - share)
-    prev_ref[:, :SLOT, :] = prev.astype(BF16)
-    prev_ref[:, SLOT:, :] = jnp.zeros((2, TILE - SLOT, TILE), BF16)
+    prev_ref[...] = prev.astype(BF16)
     own_ref[...] = own
 
 
@@ -235,7 +234,7 @@
     col = lax.broadcasted_iota(jnp.int32, (tokens, SLOT), 1)
     matrix = jnp.where((row >> 2) == col, 1.0 / POOL, 0.0).astype(BF16)
     for which, out_ref in enumerate((gk_ref, gv_ref)):
-        total = near_ref[which] + far_ref[which].astype(F32)[:SLOT]
+        total = near_ref[which] + far_ref[which].astype(F32)
         high = total.astype(BF16)
         low = (total - high.astype(F32)).astype(BF16)
         spread = dot(matrix, high) + dot(matrix, low)
@@ -319,7 +318,7 @@
     w_four = jnp.concatenate([w_pair, w_two])
     w_chip = lax.ppermute(w_four, "tm", [(c, c ^ 1) for c in range(clips)])
     back, near = call(
-        sum_body, [((2, TILE, TILE), BF16), ((2, SLOT, TILE), F32)], 2 * 10**10, 10**6, 1
+        sum_body, [((2, SLOT, TILE), BF16), ((2, SLOT, TILE), F32)], 2 * 10**10, 10**6, 1
     )(arrived)
     dost_now, _ = lax.optimization_barrier((dost, back))
     gq, direct = call(

time: 93.1 us -> 92.4 us (level)
  no operation moved by 1% of the time
where the time goes in v4:
time: 92.4 us; the launch traced here: 91.8 us
  starting transfers between devices  53.8 us (58%)
  waiting for transfers between devices  20 us (22%)
  Pallas kernels  13.4 us (15%)
  local copies, waits for them, and re-layouts  2.42 us (3%)
  between operations  1.54 us (2%)
    ppermute x1, waiting for transfers between devices, local(): far = lax.ppermute(back, 'tm', [(c + MEM, c) for c in range(clips - MEM)])  13.6 us
    ppermute x1, starting transfers between devices, local(): prev = lax.ppermute(own, 'tm', [(c, c + MEM) for c in range(clips - MEM)])  13 us
    ppermute x1, starting transfers between devices, local(): far = lax.ppermute(back, 'tm', [(c + MEM, c) for c in range(clips - MEM)])  7.04 us
    ppermute x1, starting transfers between devices, local(): theirs = lax.ppermute(other, 'head', by_four)  5.91 us
    pallas_call x1, Pallas kernels, local(): call(memory_body, [((MEM, 2, SLOT, TILE), BF16), ((2, SLOT, TILE), BF16),...  5.62 us
    all_to_all x1, starting transfers between devices, local(): memory = lax.all_to_all(outgoing, 'tm', 0, 0, axis_index_groups=groups)  4.96 us
    all_to_all x1, starting transfers between devices, local(): arrived = lax.all_to_all(payload, 'tm', 0, 0, axis_index_groups=groups)  4.86 us
    ppermute x1, starting transfers between devices, local(): a_two = lax.ppermute(a_send, 'head', by_two)  4.58 us
  transfers between devices with their start and end apart: 10, of which 5 were waited for; matrix products, arithmetic and copies ran while one was open for 0% of the time, Pallas kernels for 12%

profile of v4, /device:TPU:122, one launch (start us, length us, event | category | flops | bytes accessed | tf_op | source)
XLA Modules:
  0.0 91.8 jit_solution(1589769023425495348)
XLA Ops:
  1.3 1.8 %shard_map.93.own_ref = bf16[2,112,128]{2,1,0:T(8,128)(2,1)} custom-call(s32[1]{0:T(128)S(6)} %copy.11.start_ref, bf16[392,128]{1,0:T(8,128)(2,1)} %bitcast.18, bf16[392,128]{1,0:T(8,128)(2,1)} %bitcast.21), custom_call_target="tpu_custom_call" | custom-call | flops 10000000 | bytes 1000000 | tf_op jit(solution)/shard_map/pallas_call | solution.py:275
  3.1 13.0 %collective-permute-start = (bf16[2,112,128]{2,1,0:T(8,128)(2,1)}, bf16[2,112,128]{2,1,0:T(8,128)(2,1)S(1)}, u32[]{:S(2)}, u32[]{:S(2)}) collective-permute-start(bf16[2,112,128]{2,1,0:T(8,128)(2,1)} %shard_map.93.own_ref), channel_id=1, source_target_pairs={{0,64},{8,72},{16,80},{24,88},{32,96},{40,104},{48,112},{56,120},{... | collective-permute-start | bytes 172040 | tf_op jit(solution)/shard_map/ppermute | solution.py:280
  16.2 2.9 %collective-permute-start.1 = (bf16[64,1024]{1,0:T(8,128)(2,1)S(1)}, bf16[64,1024]{1,0:T(8,128)(2,1)S(1)}, u32[]{:S(2)}, u32[]{:S(2)}) collective-permute-start(bf16[64,1024]{1,0:T(8,128)(2,1)S(1)} %constant_dynamic-slice_fusion), channel_id=1, source_target_pairs={{0,1},{1,0},{2,3},{3,2},{4,5},{5,4},{6,7},{7,6},{8,9},{9,8},{10,11... | collective-permute-start | bytes 393224 | tf_op jit(solution)/shard_map/ppermute | solution.py:287
  19.1 0.0 copy-start.5
  19.2 1.1 %copy-done.5 = bf16[1,392,1024]{2,1,0:T(8,128)(2,1)S(1)} copy-done((bf16[1,392,1024]{2,1,0:T(8,128)(2,1)S(1)}, bf16[1,392,1024]{2,1,0:T(8,128)(2,1)}, u32[]{:S(2)}) %copy-start.5) | copy-done | bytes 802840
  20.3 0.5 shard_map.94
  20.8 0.3 copy-done.4
  21.1 0.8 shard_map.95
  21.9 1.4 %collective-permute-done.1 = bf16[64,1024]{1,0:T(8,128)(2,1)S(1)} collective-permute-done((bf16[64,1024]{1,0:T(8,128)(2,1)S(1)}, bf16[64,1024]{1,0:T(8,128)(2,1)S(1)}, u32[]{:S(2)}, u32[]{:S(2)}) %collective-permute-start.1) | collective-permute-done | bytes 131104 | tf_op jit(solution)/shard_map/ppermute | solution.py:287
  23.3 5.0 %all-to-all-start = ((bf16[8,2,112,128]{3,2,1,0:T(8,128)(2,1)}), bf16[8,2,112,128]{3,2,1,0:T(8,128)(2,1)S(1)}, u32[]{:S(2)}, u32[]{:S(2)}) async-start(bf16[8,2,112,128]{3,2,1,0:T(8,128)(2,1)} %shard_map.95), calls=%async_computation | async-start | bytes 917504 | tf_op jit(solution)/shard_map/all_to_all | solution.py:292
  28.3 0.9 copy-done
  29.2 0.0 copy-done.1
  29.2 0.8 shard_map.96
  30.0 4.4 %collective-permute-start.4 = (bf16[2,64,1024]{2,1,0:T(8,128)(2,1)S(1)}, bf16[2,64,1024]{2,1,0:T(8,128)(2,1)S(1)}, u32[]{:S(2)}, u32[]{:S(2)}) collective-permute-start(bf16[2,64,1024]{2,1,0:T(8,128)(2,1)S(1)} %pad_maximum_fusion), channel_id=1, source_target_pairs={{0,2},{1,3},{2,0},{3,1},{4,6},{5,7},{6,4},{7,5},{8,10},{9,11},{10,... | collective-permute-start | bytes 786440 | tf_op jit(solution)/shard_map/ppermute | solution.py:298
  34.4 2.0 %all-to-all-done.mem_ref = bf16[8,2,112,128]{3,2,1,0:T(8,128)(2,1)S(1)} async-done(((bf16[8,2,112,128]{3,2,1,0:T(8,128)(2,1)}), bf16[8,2,112,128]{3,2,1,0:T(8,128)(2,1)S(1)}, u32[]{:S(2)}, u32[]{:S(2)}) %all-to-all-start) | async-done | bytes 458784 | tf_op jit(solution)/shard_map/all_to_all | solution.py:292
  36.5 5.6 %shard_map.97 = (bf16[8,2,112,128]{3,2,1,0:T(8,128)(2,1)}, bf16[2,112,128]{2,1,0:T(8,128)(2,1)S(1)}, bf16[2,112,128]{2,1,0:T(8,128)(2,1)S(1)}, f32[1,896]{1,0:T(...) custom-call(s32[1]{0:T(128)S(6)} %copy.11.start_ref, ...), custom_call_target="tpu_custom_call" | custom-call | flops 4000000000 | bytes 4000000 | tf_op jit(solution)/shard_map/pallas_call | solution.py:299
  42.1 4.9 %all-to-all-start.1 = ((bf16[8,2,112,128]{3,2,1,0:T(8,128)(2,1)}), bf16[8,2,112,128]{3,2,1,0:T(8,128)(2,1)S(1)}, u32[]{:S(2)}, u32[]{:S(2)}) async-start(bf16[8,2,112,128]{3,2,1,0:T(8,128)(2,1)} %get-tuple-element.52), calls=%async_computation.1 | async-start | bytes 917504 | tf_op jit(solution)/shard_map/all_to_all | solution.py:315
  47.0 4.2 %collective-permute-start.2 = (bf16[2,112,128]{2,1,0:T(8,128)(2,1)S(1)}, bf16[2,112,128]{2,1,0:T(8,128)(2,1)S(1)}, u32[]{:S(2)}, u32[]{:S(2)}) collective-permute-start(bf16[2,112,128]{2,1,0:T(8,128)(2,1)S(1)} %get-tuple-element.55), channel_id=1, source_target_pairs={{0,1},{1,0},{2,3},{3,2},{4,5},{5,4},{6,7},{7,6},{8,9},{9,8},{10,11... | collective-permute-start | bytes 172040 | tf_op jit(solution)/shard_map/ppermute | solution.py:316
  51.2 1.9 %collective-permute-start.5 = (bf16[4,64,1024]{2,1,0:T(8,128)(2,1)S(1)}, bf16[4,64,1024]{2,1,0:T(8,128)(2,1)S(1)}, u32[]{:S(2)}, u32[]{:S(2)}) collective-permute-start(bf16[4,64,1024]{2,1,0:T(8,128)(2,1)S(1)} %constant_dynamic-update-slice_fusion.w_ref), channel_id=1, source_target_pairs={{0,8},{8,0},{16,24},{24,16},{32,40},{40,32},{48,56},{56,48},{64,72... | collective-permute-start | bytes 1572872 | tf_op jit(solution)/shard_map/ppermute | solution.py:319
  53.1 0.2 collective-permute-done.2
  53.4 4.6 %collective-permute-start.3 = (bf16[2,112,128]{2,1,0:T(8,128)(2,1)S(1)}, bf16[2,112,128]{2,1,0:T(8,128)(2,1)S(1)}, u32[]{:S(2)}, u32[]{:S(2)}) collective-permute-start(bf16[2,112,128]{2,1,0:T(8,128)(2,1)S(1)} %get-tuple-element.74), channel_id=1, source_target_pairs={{0,2},{1,3},{2,0},{3,1},{4,6},{5,7},{6,4},{7,5},{8,10},{9,11},{10,... | collective-permute-start | bytes 172040 | tf_op jit(solution)/shard_map/ppermute | solution.py:331
  57.9 0.0 all-to-all-done.1.got_ref
  58.0 0.2 shard_map.98
  58.2 2.8 %collective-permute-done.3.near_ref = bf16[2,112,128]{2,1,0:T(8,128)(2,1)S(1)} collective-permute-done((bf16[2,112,128]{2,1,0:T(8,128)(2,1)S(1)}, bf16[2,112,128]{2,1,0:T(8,128)(2,1)S(1)}, u32[]{:S(2)}, u32[]{:S(2)}) %collective-permute-start.3) | collective-permute-done | bytes 57376 | tf_op jit(solution)/shard_map/ppermute | solution.py:331
  60.9 0.8 shard_map.99
  61.7 5.9 %collective-permute-start.6 = (bf16[49,1024]{1,0:T(8,128)(2,1)S(1)}, bf16[49,1024]{1,0:T(8,128)(2,1)S(1)}, u32[]{:S(2)}, u32[]{:S(2)}) collective-permute-start(bf16[49,1024]{1,0:T(8,128)(2,1)S(1)} %get-tuple-element.62), channel_id=1, source_target_pairs={{0,4},{1,5},{2,6},{3,7},{4,0},{5,1},{6,2},{7,3},{8,12},{9,13},{10,... | collective-permute-start | bytes 301064 | tf_op jit(solution)/shard_map/ppermute | solution.py:338
  67.6 7.0 %collective-permute-start.7 = (bf16[2,112,128]{2,1,0:T(8,128)(2,1)S(1)}, bf16[2,112,128]{2,1,0:T(8,128)(2,1)S(1)}, u32[]{:S(2)}, u32[]{:S(2)}) collective-permute-start(bf16[2,112,128]{2,1,0:T(8,128)(2,1)S(1)} %get-tuple-element.71), channel_id=1, source_target_pairs={{64,0},{72,8},{80,16},{88,24},{96,32},{104,40},{112,48},{120,56},{... | collective-permute-start | bytes 172040 | tf_op jit(solution)/shard_map/ppermute | solution.py:337
  74.7 1.9 %shard_map.100 = (bf16[392,128]{1,0:T(8,128)(2,1)}, f32[2,392,128]{2,1,0:T(8,128)S(1)}) custom-call(bf16[392,128]{1,0:T(8,128)(2,1)S(1)} %bitcast.26, bf16[392,128]{1,0:T(8,128)(2,1)S(1)} %get-tuple-element.41.grad_ref, bf16[392,128]{1,0:T(8,128)(2,1)S(1)} %bitcast.20, bf16[392,128]{1,0:T(8,128)(2,1)S(1)} %bitcast.23, ...), custom_call_target="tpu_custom_call" | custom-call | flops 10000 | bytes 10000 | tf_op jit(solution)/shard_map/pallas_call | solution.py:324
  76.5 13.6 %collective-permute-done.7.far_ref = bf16[2,112,128]{2,1,0:T(8,128)(2,1)S(1)} collective-permute-done((bf16[2,112,128]{2,1,0:T(8,128)(2,1)S(1)}, bf16[2,112,128]{2,1,0:T(8,128)(2,1)S(1)}, u32[]{:S(2)}, u32[]{:S(2)}) %collective-permute-start.7) | collective-permute-done | bytes 57376 | tf_op jit(solution)/shard_map/ppermute | solution.py:337
  90.1 1.0 %shard_map.101 = (bf16[392,128]{1,0:T(8,128)(2,1)}, bf16[392,128]{1,0:T(8,128)(2,1)}) custom-call(f32[2,392,128]{2,1,0:T(8,128)S(1)} %get-tuple-element.69.direct_ref, f32[2,112,128]{2,1,0:T(8,128)S(1)} %get-tuple-element.70.near_ref, bf16[2,112,128]{2,1,0:T(8,128)(2,1)S(1)} %collective-permute-done.7.far_ref), custom_call_target="tpu_custom_call" | custom-call | flops 10000 | bytes 10000 | tf_op jit(solution)/shard_map/pallas_call | solution.py:340
  91.1 0.0 collective-permute-done.6
  91.1 0.7 fusion
  (16 shorter events, 0.1 us)
Async XLA Ops:
  0.6 15.6 %copy-start.2 = (bf16[128,1024]{1,0:T(8,128)(2,1)S(1)}, bf16[128,1024]{1,0:T(8,128)(2,1)}, u32[]{:S(2)}) copy-start(bf16[128,1024]{1,0:T(8,128)(2,1)} %w_ref.1) | copy-start | bytes 786436
  3.1 17.7 %collective-permute-start = (bf16[2,112,128]{2,1,0:T(8,128)(2,1)}, bf16[2,112,128]{2,1,0:T(8,128)(2,1)S(1)}, u32[]{:S(2)}, u32[]{:S(2)}) collective-permute-start(bf16[2,112,128]{2,1,0:T(8,128)(2,1)} %shard_map.93.own_ref), channel_id=1, source_target_pairs={{0,64},{8,72},{16,80},{24,88},{32,96},{40,104},{48,112},{56,120},{... | collective-permute-start | bytes 172040 | tf_op jit(solution)/shard_map/ppermute | solution.py:280
  16.2 7.1 %collective-permute-start.1 = (bf16[64,1024]{1,0:T(8,128)(2,1)S(1)}, bf16[64,1024]{1,0:T(8,128)(2,1)S(1)}, u32[]{:S(2)}, u32[]{:S(2)}) collective-permute-start(bf16[64,1024]{1,0:T(8,128)(2,1)S(1)} %constant_dynamic-slice_fusion), channel_id=1, source_target_pairs={{0,1},{1,0},{2,3},{3,2},{4,5},{5,4},{6,7},{7,6},{8,9},{9,8},{10,11... | collective-permute-start | bytes 393224 | tf_op jit(solution)/shard_map/ppermute | solution.py:287
  19.1 1.1 %copy-start.5 = (bf16[1,392,1024]{2,1,0:T(8,128)(2,1)S(1)}, bf16[1,392,1024]{2,1,0:T(8,128)(2,1)}, u32[]{:S(2)}) copy-start(bf16[1,392,1024]{2,1,0:T(8,128)(2,1)} %param.10) | copy-start | bytes 2408452
  20.3 0.8 copy-start.4
  23.3 5.0 %copy-start.3 = (bf16[1,392,128]{2,1,0:T(8,128)(2,1)S(1)}, bf16[1,392,128]{2,1,0:T(8,128)(2,1)}, u32[]{:S(2)}) copy-start(bf16[1,392,128]{2,1,0:T(8,128)(2,1)} %param.6) | copy-start | bytes 301060
  23.3 13.2 %all-to-all-start = ((bf16[8,2,112,128]{3,2,1,0:T(8,128)(2,1)}), bf16[8,2,112,128]{3,2,1,0:T(8,128)(2,1)S(1)}, u32[]{:S(2)}, u32[]{:S(2)}) async-start(bf16[8,2,112,128]{3,2,1,0:T(8,128)(2,1)} %shard_map.95), calls=%async_computation | async-start | bytes 917504 | tf_op jit(solution)/shard_map/all_to_all | solution.py:292
  28.3 0.9 copy-start
  28.3 0.9 %copy-start.1 = (bf16[1,392,128]{2,1,0:T(8,128)(2,1)S(1)}, bf16[1,392,128]{2,1,0:T(8,128)(2,1)}, u32[]{:S(2)}) copy-start(bf16[1,392,128]{2,1,0:T(8,128)(2,1)} %param.8) | copy-start | bytes 301060
  30.0 16.9 %collective-permute-start.4 = (bf16[2,64,1024]{2,1,0:T(8,128)(2,1)S(1)}, bf16[2,64,1024]{2,1,0:T(8,128)(2,1)S(1)}, u32[]{:S(2)}, u32[]{:S(2)}) collective-permute-start(bf16[2,64,1024]{2,1,0:T(8,128)(2,1)S(1)} %pad_maximum_fusion), channel_id=1, source_target_pairs={{0,2},{1,3},{2,0},{3,1},{4,6},{5,7},{6,4},{7,5},{8,10},{9,11},{10,... | collective-permute-start | bytes 786440 | tf_op jit(solution)/shard_map/ppermute | solution.py:298
  42.1 15.9 %all-to-all-start.1 = ((bf16[8,2,112,128]{3,2,1,0:T(8,128)(2,1)}), bf16[8,2,112,128]{3,2,1,0:T(8,128)(2,1)S(1)}, u32[]{:S(2)}, u32[]{:S(2)}) async-start(bf16[8,2,112,128]{3,2,1,0:T(8,128)(2,1)} %get-tuple-element.52), calls=%async_computation.1 | async-start | bytes 917504 | tf_op jit(solution)/shard_map/all_to_all | solution.py:315
  47.0 6.4 %collective-permute-start.2 = (bf16[2,112,128]{2,1,0:T(8,128)(2,1)S(1)}, bf16[2,112,128]{2,1,0:T(8,128)(2,1)S(1)}, u32[]{:S(2)}, u32[]{:S(2)}) collective-permute-start(bf16[2,112,128]{2,1,0:T(8,128)(2,1)S(1)} %get-tuple-element.55), channel_id=1, source_target_pairs={{0,1},{1,0},{2,3},{3,2},{4,5},{5,4},{6,7},{7,6},{8,9},{9,8},{10,11... | collective-permute-start | bytes 172040 | tf_op jit(solution)/shard_map/ppermute | solution.py:316
  51.2 9.7 %collective-permute-start.5 = (bf16[4,64,1024]{2,1,0:T(8,128)(2,1)S(1)}, bf16[4,64,1024]{2,1,0:T(8,128)(2,1)S(1)}, u32[]{:S(2)}, u32[]{:S(2)}) collective-permute-start(bf16[4,64,1024]{2,1,0:T(8,128)(2,1)S(1)} %constant_dynamic-update-slice_fusion.w_ref), channel_id=1, source_target_pairs={{0,8},{8,0},{16,24},{24,16},{32,40},{40,32},{48,56},{56,48},{64,72... | collective-permute-start | bytes 1572872 | tf_op jit(solution)/shard_map/ppermute | solution.py:319
  53.4 7.6 %collective-permute-start.3 = (bf16[2,112,128]{2,1,0:T(8,128)(2,1)S(1)}, bf16[2,112,128]{2,1,0:T(8,128)(2,1)S(1)}, u32[]{:S(2)}, u32[]{:S(2)}) collective-permute-start(bf16[2,112,128]{2,1,0:T(8,128)(2,1)S(1)} %get-tuple-element.74), channel_id=1, source_target_pairs={{0,2},{1,3},{2,0},{3,1},{4,6},{5,7},{6,4},{7,5},{8,10},{9,11},{10,... | collective-permute-start | bytes 172040 | tf_op jit(solution)/shard_map/ppermute | solution.py:331
  61.7 29.4 %collective-permute-start.6 = (bf16[49,1024]{1,0:T(8,128)(2,1)S(1)}, bf16[49,1024]{1,0:T(8,128)(2,1)S(1)}, u32[]{:S(2)}, u32[]{:S(2)}) collective-permute-start(bf16[49,1024]{1,0:T(8,128)(2,1)S(1)} %get-tuple-element.62), channel_id=1, source_target_pairs={{0,4},{1,5},{2,6},{3,7},{4,0},{5,1},{6,2},{7,3},{8,12},{9,13},{10,... | collective-permute-start | bytes 301064 | tf_op jit(solution)/shard_map/ppermute | solution.py:338
  67.6 22.5 %collective-permute-start.7 = (bf16[2,112,128]{2,1,0:T(8,128)(2,1)S(1)}, bf16[2,112,128]{2,1,0:T(8,128)(2,1)S(1)}, u32[]{:S(2)}, u32[]{:S(2)}) collective-permute-start(bf16[2,112,128]{2,1,0:T(8,128)(2,1)S(1)} %get-tuple-element.71), channel_id=1, source_target_pairs={{64,0},{72,8},{80,16},{88,24},{96,32},{104,40},{112,48},{120,56},{... | collective-permute-start | bytes 172040 | tf_op jit(solution)/shard_map/ppermute | solution.py:337
